TPU v7x, 128 devices: a whole 4x4x4 slice. The times are simulated.
128 devices in a mesh: az: 32 (over y_lo, x, z), ax: 4 (over y_hi, core).
Axes of the slice: x: 4, y: 4 (y_hi: 2, y_lo: 2; y = y_hi * 2 + y_lo), z: 4, core: 2. Of those that a mesh axis runs over, the one named last changes fastest.
Arguments:
- initial: float32 [512, 64, 512], P('az', 'ax'), may hold values from -6 to 6
- target: float32 [512, 64, 512], P('az', 'ax'), may hold values from -6 to 6
- basis: float32 [16, 64, 512], P(None, 'ax'), may hold values from -0.25 to 0.25
- coefficients: float32 [16], replicated, may hold values from -4 to 4
- blade: float32 [2, 512], P(None, 'az'), may hold values from 0.3 to 3
- offset: int32 [2], replicated, may hold values from 256 to 511, as said below
- extra: int32 [2, 512], P(None, 'az'), may hold values from 0 to 1
- frac: float32 [2, 512], P(None, 'az'), may hold values from 0 to 1
Outputs:
- final_field: float32 [512, 64, 512], P('az', 'ax')
- sensitivity: float32 [512, 64, 512], P('az', 'ax')
- gradient: float32 [16], replicated
- loss: float32 [], replicated
Inputs may be any that keep to these rules, and one draw needn't show every extreme that they name: offset[0] lies in 256 to 271; offset[1] is 511.
All inputs are finite; a program needn't handle non-finite values.
Results may differ from a plain program's by a relative error of at most 0.00018.
Values sent between devices are 32-bit elements; how exact they have to be, the bound alone decides.
A program may use at most 64 MiB of HBM per device.

v0:
```python
import jax
import jax.numpy as jnp
from jax import lax
from jax.sharding import PartitionSpec as P

diffusion = 0.12
advection = 0.2
coupling = 0.12


def extended(array, sides, width, wrap):
    for axis, dim in sides:
        size, length = (lax.axis_size(axis), array.shape[dim])
        up = [(i, (i + 1) % size) for i in range(size if wrap else size - 1)]
        down = [(j, i) for i, j in up]
        last = lax.slice_in_dim(array, length - width, length, axis=dim)
        leading = lax.slice_in_dim(array, 0, width, axis=dim)
        before = lax.ppermute(last, axis, up)
        after = lax.ppermute(leading, axis, down)
        array = jnp.concatenate([before, array, after], axis=dim)
    return array


def radial_term(field, split):
    padded = jnp.pad(field, ((0, 0), (0, 0), (1, 1)))
    faces = padded[:, :, 1:] - padded[:, :, :-1]
    keep = (jnp.arange(field.shape[2] + 1, dtype=jnp.int32) != split).astype(jnp.float32)
    faces = faces * keep
    return faces[:, :, 1:] - faces[:, :, :-1]


def interface(stator, rotor, shift_cells, extra_row, weight):
    blocks = stator.shape[0]
    width = stator.shape[1]
    cycle = lax.all_gather(stator, "az", axis=0, tiled=True)
    total = cycle.shape[0]
    cells = lax.axis_index("az") * blocks + jnp.arange(blocks, dtype=jnp.int32)
    first = (cells + shift_cells + extra_row) % total
    second = (first + 1) % total
    flux = (1.0 - weight) * cycle[first] + weight * cycle[second] - rotor
    spread = (
        jnp.zeros((total, width), jnp.float32)
        .at[first]
        .add((1.0 - weight) * flux)
        .at[second]
        .add(weight * flux)
    )
    back = lax.psum_scatter(spread, "az", scatter_dimension=0, tiled=True)
    return (flux, back)


def operator(field, step, offset, extra, frac, forward):
    split = field.shape[2] // 2
    beside_all = extended(field, (("az", 0),), 1, True)
    along = extended(field, (("ax", 1),), 1, False)
    lap = (
        beside_all[2:]
        + beside_all[:-2]
        + along[:, 2:]
        + along[:, :-2]
        - 4.0 * field
        + radial_term(field, split)
    )
    if forward:
        adv = field - beside_all[:-2]
    else:
        adv = field - beside_all[2:]
    flux, back = interface(
        field[:, :, split], field[:, :, split - 1], offset[step], extra[step], frac[step][:, None]
    )
    result = diffusion * lap - advection * adv
    result = result.at[:, :, split - 1].add(coupling * flux)
    result = result.at[:, :, split].add(-coupling * back)
    return result


def on_device(initial, target, basis, coefficients, blade, offset, extra, frac):
    steps_count = blade.shape[0]
    profile = jnp.tensordot(coefficients, basis, axes=1, precision=lax.Precision.HIGHEST)
    field = initial
    for step in range(steps_count):
        source = blade[step][:, None, None] * profile[None]
        field = field + operator(field, step, offset, extra, frac, True) + source
    misfit = field - target
    local_loss = 0.5 * jnp.sum(misfit * misfit)
    loss_total = lax.psum(local_loss, ("az", "ax"))
    adjoint = misfit
    grad_local = jnp.zeros((basis.shape[0],), jnp.float32)
    for step in reversed(range(steps_count)):
        weighted = jnp.tensordot(blade[step], adjoint, axes=(0, 0), precision=lax.Precision.HIGHEST)
        grad_local = grad_local + jnp.tensordot(
            basis, weighted, axes=((1, 2), (0, 1)), precision=lax.Precision.HIGHEST
        )
        adjoint = adjoint + operator(adjoint, step, offset, extra, frac, False)
    grad_total = lax.psum(grad_local, ("az", "ax"))
    columns = field.shape[0] * lax.axis_size("az") * field.shape[1] * lax.axis_size("ax")
    gradient = grad_total / columns
    loss = loss_total / (columns * field.shape[2])
    return (field, adjoint, gradient, loss)


def solution(mesh):
    in_specs = (
        P("az", "ax", None),
        P("az", "ax", None),
        P(None, "ax", None),
        P(),
        P(None, "az"),
        P(),
        P(None, "az"),
        P(None, "az"),
    )
    out_specs = (P("az", "ax", None), P("az", "ax", None), P(), P())
    return jax.shard_map(
        on_device, mesh=mesh, in_specs=in_specs, out_specs=out_specs, check_vma=False
    )
```

profile of v0, /device:TPU:0, one launch (start us, length us, event | category | flops | bytes accessed | tf_op | source)
XLA Modules:
  0.0 1083.0 jit_solution(16937462357210216996)
XLA Ops:
  9.8 1.3 fusion.90
  11.2 1.2 slice_reduce_fusion.3
  12.5 84.0 %all-gather = f32[512,16,1]{1,0,2:T(8,128)S(1)} all-gather(f32[16,16,1]{1,0,2:T(8,128)S(1)} %copy.567), channel_id=2, replica_groups=mesh['az'=32,'ax'=4] {'az'}, dimensions={0}, use_global_device_ids=true | all-gather | bytes 33792 | tf_op jit(solution)/shard_map/all_gather | solution.py:35
  97.6 0.8 scatter_custom_fusion
  98.4 0.9 scatter_custom_fusion.1
  100.2 1.3 collective-permute-start.2
  101.5 3.0 collective-permute-start.3
  104.6 2.0 collective-permute-start.1
  109.1 3.7 collective-permute-done.1
  113.3 1.2 scatter-add.96
  114.6 141.3 %reduce-scatter.5.cloned.1.call-done = f32[16,16]{1,0:T(8,128)} async-done(((f32[512,16]{1,0:T(8,128)}), f32[16,16]{1,0:T(8,128)}) %reduce-scatter.5.cloned.1.call-update) | async-done | bytes 1040 | tf_op jit(solution)/shard_map/reduce_scatter | solution.py:48
  255.9 0.7 multiply_bitcast_fusion.3
  257.5 1.3 collective-permute-start.6
  258.8 3.0 collective-permute-start.7
  261.8 0.9 collective-permute-start.4
  262.8 1.2 collective-permute-start.5
  264.3 81.7 %all-gather.1 = f32[512,16,1]{1,2,0:T(1,128)S(1)} all-gather(f32[16,16,1]{1,2,0:T(1,128)S(1)} %copy.522), channel_id=3, replica_groups=mesh['az'=32,'ax'=4] {'az'}, dimensions={0}, use_global_device_ids=true | all-gather | bytes 33792 | tf_op jit(solution)/shard_map/all_gather | solution.py:35
  347.1 0.8 scatter_custom_fusion.2
  347.9 0.9 scatter_custom_fusion.3
  350.5 1.2 scatter-add.100
  351.8 154.1 %reduce-scatter.7.cloned.1.call-done = f32[16,16]{1,0:T(8,128)} async-done(((f32[512,16]{1,0:T(8,128)}), f32[16,16]{1,0:T(8,128)}) %reduce-scatter.7.cloned.1.call-update) | async-done | bytes 1040 | tf_op jit(solution)/shard_map/reduce_scatter | solution.py:48
  505.9 0.7 multiply_bitcast_fusion.2
  507.0 1.5 multiply_reduce_fusion
  508.9 1.3 collective-permute-start.10
  510.2 3.0 collective-permute-start.11
  513.2 0.8 collective-permute-start.8
  514.0 1.3 collective-permute-start.9
  515.3 0.7 fusion.47
  516.2 81.6 %all-gather.2 = f32[512,16,1]{1,2,0:T(1,128)S(1)} all-gather(f32[16,16,1]{1,2,0:T(1,128)S(1)} %copy.533), channel_id=4, replica_groups=mesh['az'=32,'ax'=4] {'az'}, dimensions={0}, use_global_device_ids=true | all-gather | bytes 33792 | tf_op jit(solution)/shard_map/all_gather | solution.py:35
  600.0 0.8 scatter_custom_fusion.4
  600.8 0.9 scatter_custom_fusion.5
  602.6 0.9 convolution_bitcast_fusion.1
  604.2 1.2 scatter-add.104
  605.4 153.0 %reduce-scatter.9.cloned.1.call-done = f32[16,16]{1,0:T(8,128)} async-done(((f32[512,16]{1,0:T(8,128)}), f32[16,16]{1,0:T(8,128)}) %reduce-scatter.9.cloned.1.call-update) | async-done | bytes 1040 | tf_op jit(solution)/shard_map/reduce_scatter | solution.py:48
  758.4 0.7 multiply_bitcast_fusion.1
  760.8 1.3 collective-permute-start.14
  762.1 3.0 collective-permute-start.15
  765.2 0.8 collective-permute-start.12
  766.0 0.9 fusion
  767.0 1.3 collective-permute-start.13
  768.3 65.7 %all-reduce.4 = (f32[16]{0:T(128)S(1)}, f32[]{:T(128)}) all-reduce(f32[16]{0:T(128)S(1)} %fusion, f32[]{:T(128)S(6)} %mul_shard_map.3), channel_id=1, replica_groups=mesh['az'=32,'ax'=4] {'az','ax'}, use_global_device_ids=true, to_apply=%region_12.13 | all-reduce | flops 17 | bytes 136 | tf_op jit(solution)/shard_map/psum | solution.py:95
  834.7 80.4 %all-gather.3 = f32[512,16,1]{1,2,0:T(1,128)S(1)} all-gather(f32[16,16,1]{1,2,0:T(1,128)S(1)} %copy.544), channel_id=5, replica_groups=mesh['az'=32,'ax'=4] {'az'}, dimensions={0}, use_global_device_ids=true | all-gather | bytes 33792 | tf_op jit(solution)/shard_map/all_gather | solution.py:35
  916.2 0.8 scatter_custom_fusion.6
  917.0 0.9 scatter_custom_fusion.7
  920.2 1.2 scatter-add.108
  921.5 151.9 %reduce-scatter.11.cloned.1.call-done = f32[16,16]{1,0:T(8,128)} async-done(((f32[512,16]{1,0:T(8,128)}), f32[16,16]{1,0:T(8,128)}) %reduce-scatter.11.cloned.1.call-update) | async-done | bytes 1040 | tf_op jit(solution)/shard_map/reduce_scatter | solution.py:48
  1073.4 0.7 multiply_bitcast_fusion
  1074.4 0.9 add.491
  (138 shorter events, 21.1 us)
Async XLA Ops:
  7.2 100.2 %copy-start = (f32[16,16,512]{2,1,0:T(8,128)S(1)}, f32[16,16,512]{2,1,0:T(8,128)}, u32[]{:S(2)}) copy-start(f32[16,16,512]{2,1,0:T(8,128)} %param.26) | copy-start | bytes 1572868
  7.2 0.7 copy-start.8
  7.2 248.8 %reduce-scatter.5.cloned.1.call-start = ((), (), s32[]{:S(2)}) async-start(), calls=%async_computation.4 | async-start | bytes 270336 | tf_op jit(solution)/shard_map/reduce_scatter | solution.py:48
  7.9 0.7 copy-start.9
  9.2 0.7 copy-start.10
  96.5 3.6 copy-start.1
  99.3 0.7 copy-start.4
  100.0 405.9 %reduce-scatter.7.cloned.1.call-start = ((), (), s32[]{:S(2)}) async-start(), calls=%async_computation.5 | async-start | bytes 270336 | tf_op jit(solution)/shard_map/reduce_scatter | solution.py:48
  100.2 8.8 collective-permute-start.2
  101.5 7.6 collective-permute-start.3
  104.5 4.6 collective-permute-start
  104.6 8.2 collective-permute-start.1
  106.6 0.7 copy-start.7
  107.3 0.7 copy-start.11
  257.5 92.4 %collective-permute-start.6 = (f32[16,1,512]{2,0,1:T(8,128)S(1)}, f32[16,1,512]{2,0,1:T(8,128)S(1)}, u32[]{:S(2)}, u32[]{:S(2)}) collective-permute-start(f32[16,1,512]{2,0,1:T(8,128)S(1)} %copy.518), channel_id=1, source_target_pairs={{1,0},{2,1},{3,2},{5,4},{6,5},{7,6},{9,8},{10,9},{11,10},{13,12},{... | collective-permute-start | bytes 98312 | tf_op jit(solution)/shard_map/ppermute | solution.py:19
  258.8 91.1 %collective-permute-start.7 = (f32[16,1,512]{2,0,1:T(8,128)S(1)}, f32[16,1,512]{2,0,1:T(8,128)S(1)}, u32[]{:S(2)}, u32[]{:S(2)}) collective-permute-start(f32[16,1,512]{2,0,1:T(8,128)S(1)} %copy.520), channel_id=1, source_target_pairs={{0,1},{1,2},{2,3},{4,5},{5,6},{6,7},{8,9},{9,10},{10,11},{12,13},{... | collective-permute-start | bytes 98312 | tf_op jit(solution)/shard_map/ppermute | solution.py:18
  261.8 88.1 %collective-permute-start.4 = (f32[1,16,512]{2,1,0:T(8,128)S(1)}, f32[1,16,512]{2,1,0:T(8,128)S(1)}, u32[]{:S(2)}, u32[]{:S(2)}) collective-permute-start(f32[1,16,512]{2,1,0:T(8,128)S(1)} %get-tuple-element.135), channel_id=1, source_target_pairs={{4,0},{8,4},{12,8},{16,12},{20,16},{24,20},{28,24},{32,28},{36,32}... | collective-permute-start | bytes 98312 | tf_op jit(solution)/shard_map/ppermute | solution.py:19
  262.8 87.2 %collective-permute-start.5 = (f32[1,16,512]{2,1,0:T(8,128)S(1)}, f32[1,16,512]{2,1,0:T(8,128)S(1)}, u32[]{:S(2)}, u32[]{:S(2)}) collective-permute-start(f32[1,16,512]{2,1,0:T(8,128)S(1)} %get-tuple-element.136), channel_id=1, source_target_pairs={{0,4},{4,8},{8,12},{12,16},{16,20},{20,24},{24,28},{28,32},{32,36}... | collective-permute-start | bytes 98312 | tf_op jit(solution)/shard_map/ppermute | solution.py:18
  348.7 0.7 copy-start.5
  349.5 408.9 %reduce-scatter.9.cloned.1.call-start = ((), (), s32[]{:S(2)}) async-start(), calls=%async_computation.6 | async-start | bytes 270336 | tf_op jit(solution)/shard_map/reduce_scatter | solution.py:48
  350.5 156.4 %copy-start.6 = (f32[16,16,512]{2,1,0:T(8,128)S(1)}, f32[16,16,512]{2,1,0:T(8,128)}, u32[]{:S(2)}) copy-start(f32[16,16,512]{2,1,0:T(8,128)} %param.25) | copy-start | bytes 1572868
  508.9 90.4 %collective-permute-start.10 = (f32[16,1,512]{2,0,1:T(8,128)S(1)}, f32[16,1,512]{2,0,1:T(8,128)S(1)}, u32[]{:S(2)}, u32[]{:S(2)}) collective-permute-start(f32[16,1,512]{2,0,1:T(8,128)S(1)} %copy.529), channel_id=1, source_target_pairs={{1,0},{2,1},{3,2},{5,4},{6,5},{7,6},{9,8},{10,9},{11,10},{13,12},{... | collective-permute-start | bytes 98312 | tf_op jit(solution)/shard_map/ppermute | solution.py:19
  510.2 89.1 %collective-permute-start.11 = (f32[16,1,512]{2,0,1:T(8,128)S(1)}, f32[16,1,512]{2,0,1:T(8,128)S(1)}, u32[]{:S(2)}, u32[]{:S(2)}) collective-permute-start(f32[16,1,512]{2,0,1:T(8,128)S(1)} %copy.531), channel_id=1, source_target_pairs={{0,1},{1,2},{2,3},{4,5},{5,6},{6,7},{8,9},{9,10},{10,11},{12,13},{... | collective-permute-start | bytes 98312 | tf_op jit(solution)/shard_map/ppermute | solution.py:18
  513.2 86.1 %collective-permute-start.8 = (f32[1,16,512]{2,1,0:T(8,128)S(1)}, f32[1,16,512]{2,1,0:T(8,128)S(1)}, u32[]{:S(2)}, u32[]{:S(2)}) collective-permute-start(f32[1,16,512]{2,1,0:T(8,128)S(1)} %get-tuple-element.129), channel_id=1, source_target_pairs={{4,0},{8,4},{12,8},{16,12},{20,16},{24,20},{28,24},{32,28},{36,32}... | collective-permute-start | bytes 98312 | tf_op jit(solution)/shard_map/ppermute | solution.py:19
  514.0 85.3 %collective-permute-start.9 = (f32[1,16,512]{2,1,0:T(8,128)S(1)}, f32[1,16,512]{2,1,0:T(8,128)S(1)}, u32[]{:S(2)}, u32[]{:S(2)}) collective-permute-start(f32[1,16,512]{2,1,0:T(8,128)S(1)} %get-tuple-element.130), channel_id=1, source_target_pairs={{0,4},{4,8},{8,12},{12,16},{16,20},{20,24},{24,28},{28,32},{32,36}... | collective-permute-start | bytes 98312 | tf_op jit(solution)/shard_map/ppermute | solution.py:18
  601.6 0.7 copy-start.2
  602.4 471.0 %reduce-scatter.11.cloned.1.call-start = ((), (), s32[]{:S(2)}) async-start(), calls=%async_computation.7 | async-start | bytes 270336 | tf_op jit(solution)/shard_map/reduce_scatter | solution.py:48
  760.8 158.7 %collective-permute-start.14 = (f32[16,1,512]{2,0,1:T(8,128)S(1)}, f32[16,1,512]{2,0,1:T(8,128)S(1)}, u32[]{:S(2)}, u32[]{:S(2)}) collective-permute-start(f32[16,1,512]{2,0,1:T(8,128)S(1)} %copy.540), channel_id=1, source_target_pairs={{1,0},{2,1},{3,2},{5,4},{6,5},{7,6},{9,8},{10,9},{11,10},{13,12},{... | collective-permute-start | bytes 98312 | tf_op jit(solution)/shard_map/ppermute | solution.py:19
  762.1 157.5 %collective-permute-start.15 = (f32[16,1,512]{2,0,1:T(8,128)S(1)}, f32[16,1,512]{2,0,1:T(8,128)S(1)}, u32[]{:S(2)}, u32[]{:S(2)}) collective-permute-start(f32[16,1,512]{2,0,1:T(8,128)S(1)} %copy.542), channel_id=1, source_target_pairs={{0,1},{1,2},{2,3},{4,5},{5,6},{6,7},{8,9},{9,10},{10,11},{12,13},{... | collective-permute-start | bytes 98312 | tf_op jit(solution)/shard_map/ppermute | solution.py:18
  765.2 154.5 %collective-permute-start.12 = (f32[1,16,512]{2,1,0:T(8,128)S(1)}, f32[1,16,512]{2,1,0:T(8,128)S(1)}, u32[]{:S(2)}, u32[]{:S(2)}) collective-permute-start(f32[1,16,512]{2,1,0:T(8,128)S(1)} %get-tuple-element.123), channel_id=1, source_target_pairs={{4,0},{8,4},{12,8},{16,12},{20,16},{24,20},{28,24},{32,28},{36,32}... | collective-permute-start | bytes 98312 | tf_op jit(solution)/shard_map/ppermute | solution.py:19
  767.0 152.7 %collective-permute-start.13 = (f32[1,16,512]{2,1,0:T(8,128)S(1)}, f32[1,16,512]{2,1,0:T(8,128)S(1)}, u32[]{:S(2)}, u32[]{:S(2)}) collective-permute-start(f32[1,16,512]{2,1,0:T(8,128)S(1)} %get-tuple-element.124), channel_id=1, source_target_pairs={{0,4},{4,8},{8,12},{12,16},{16,20},{20,24},{24,28},{28,32},{32,36}... | collective-permute-start | bytes 98312 | tf_op jit(solution)/shard_map/ppermute | solution.py:18
  917.8 0.7 copy-start.3
Sparse Core Ops, SparseCore 0:
  100.2 155.7 reduce-scatter.4
  349.6 156.2 reduce-scatter.6
  602.5 155.8 reduce-scatter.8
  918.7 154.6 reduce-scatter.10
where the time goes:
time: 1080 us
  waiting for transfers between devices  604 us (56%)
  blocking collectives  393 us (36%)
  starting transfers between devices  26.1 us (2%)
  local copies, waits for them, and re-layouts  21.3 us (2%)
  other arithmetic  17.1 us (2%)
  between operations  17 us (2%)
    reduce_scatter x4, waiting for transfers between devices, interface(): back = lax.psum_scatter(spread, 'az', scatter_dimension=0, tiled=True)  600 us
    all_gather x4, blocking collectives, interface(): cycle = lax.all_gather(stator, 'az', axis=0, tiled=True)  328 us
    psum x1, blocking collectives, on_device(): grad_total = lax.psum(grad_local, ('az', 'ax'))  65.7 us
  transfers between devices with their start and end apart: 20, of which 5 were waited for; matrix products, arithmetic and copies ran while one was open for 2% of the time, Pallas kernels for 0%

commit v1 on v0

v1 whole, which is shorter than its diff:
```python
import functools

import jax
import jax.numpy as jnp
from jax import lax
from jax.experimental import pallas as pl
from jax.experimental.pallas import tpu as pltpu
from jax.sharding import PartitionSpec as P

MESH = pl.DeviceIdType.MESH
f32 = jnp.float32
HI = lax.Precision.HIGHEST

NA, NX = 32, 4
J, Z, R, M = 16, 16, 512, 16
RI = 256
DIFF, ADV = 0.12, 0.2
COLUMNS = NA * J * NX * Z

NEAR = [(a, c) for a in (-1, 0, 1) for c in (-1, 0, 1) if (a, c) != (0, 0)]
FAR = [(a, c) for a in (14, 15, 16, 17, 18) for c in (-1, 0, 1)]
PARTNERS = FAR + NEAR


def slot_of(a, c):
    return [((x + 8) % NA, y) for x, y in PARTNERS].index(((a + 8) % NA, c))


def lane_iota(shape):
    return lax.broadcasted_iota(jnp.int32, shape, len(shape) - 1)


def row_iota(shape):
    return lax.broadcasted_iota(jnp.int32, shape, len(shape) - 2)


def left(v):
    return pltpu.roll(v, v.shape[-1] - 1, v.ndim - 1)


def right(v):
    return pltpu.roll(v, 1, v.ndim - 1)


def kernel(
    u_h, t_h, basis_h, coef_h, blade_h, off_h, extra_h, frac_h,
    fin, sen, tot,
    x0, u1, l2, l1, tg, bs, bh, prof, m1s, m1r, m2s, m2r, rrs, rrr, bb,
    blade_v, extra_v, frac_v, coef_s, off_s,
    loc, near_ss, near_rs, m_ss, m_rs, side_ss, side_rs, rr_ss, rr_rs,
):
    az, ax = lax.axis_index("az"), lax.axis_index("ax")
    me = az * NX + ax

    def partner(a, c):
        return (lax.rem(az + a + NA, NA), lax.rem(ax + c + NX, NX))

    def ranked(k):
        t = lax.rem(me + k, NA * NX)
        return (t // NX, lax.rem(t, NX))

    barrier = pltpu.get_barrier_semaphore()

    def greet(k, _):
        pl.semaphore_signal(barrier, inc=1, device_id=ranked(k + 1), device_id_type=MESH)
        return 0

    lax.fori_loop(0, NA * NX - 1, greet, 0)

    loads = [
        pltpu.make_async_copy(u_h, x0.at[2:18, 8:24, :], loc.at[0]),
        pltpu.make_async_copy(basis_h, bs, loc.at[1]),
        pltpu.make_async_copy(coef_h, coef_s, loc.at[2]),
        pltpu.make_async_copy(off_h, off_s, loc.at[3]),
        pltpu.make_async_copy(blade_h, blade_v, loc.at[4]),
        pltpu.make_async_copy(extra_h, extra_v, loc.at[5]),
        pltpu.make_async_copy(frac_h, frac_v, loc.at[6]),
        pltpu.make_async_copy(t_h, tg, loc.at[7]),
    ]
    for c in loads:
        c.start()

    m1s[...] = jnp.zeros((24, 128), f32)
    for c in loads:
        c.wait()
    lane = lane_iota((Z, 128))

    def take(j, carry):
        rot, sta = carry
        a = pltpu.roll(x0[j + 2, 8:24, 128:256], j + 1, 1)
        b = pltpu.roll(x0[j + 2, 8:24, 256:384], j + 16, 1)
        return jnp.where(lane == j, a, rot), jnp.where(lane == j + 16, b, sta)

    zero = jnp.zeros((Z, 128), f32)
    rot, sta = lax.fori_loop(0, J, take, (zero, zero))
    m1s[0:16, :] = rot + sta
    m1s[16:18, 0:16] = extra_v[...].astype(f32)
    m1s[18:20, 0:16] = frac_v[...]
    m1s[20:22, 0:16] = blade_v[...]

    def mix(m, acc):
        return acc + coef_s[m] * bs[m]

    prof[8:24, :] = lax.fori_loop(0, M, mix, jnp.zeros((Z, R), f32))

    pl.semaphore_wait(barrier, NA * NX - 1)

    plane_src = {-1: pl.ds(0, 2), 0: pl.ds(0, 16), 1: pl.ds(14, 2)}
    row_src = {-1: pl.ds(0, 2), 0: pl.ds(0, 16), 1: pl.ds(14, 2)}
    plane_dst = {-1: pl.ds(18, 2), 0: pl.ds(2, 16), 1: pl.ds(0, 2)}
    row_dst = {-1: pl.ds(24, 2), 0: pl.ds(8, 16), 1: pl.ds(6, 2)}
    plane_own = {-1: pl.ds(2, 2), 0: pl.ds(2, 16), 1: pl.ds(16, 2)}
    row_own = {-1: pl.ds(8, 2), 0: pl.ds(8, 16), 1: pl.ds(22, 2)}

    def near_copy(src, dst, a, c, n):
        i = NEAR.index((a, c))
        return pltpu.make_async_remote_copy(
            src_ref=src, dst_ref=dst.at[plane_dst[a], row_dst[c], :],
            send_sem=near_ss.at[n, i], recv_sem=near_rs.at[n, i],
            device_id=partner(a, c), device_id_type=MESH,
        )

    def message(src, dst, a, c, n):
        return pltpu.make_async_remote_copy(
            src_ref=src, dst_ref=dst.at[slot_of(-a, -c)],
            send_sem=m_ss.at[n], recv_sem=m_rs.at[n],
            device_id=partner(a, c), device_id_type=MESH,
        )

    first = [near_copy(u_h.at[plane_src[a], row_src[c], :], x0, a, c, 0) for a, c in NEAR]
    far1 = [message(m1s, m1r, a, c, 0) for a, c in PARTNERS]
    side = []
    for i, (c, src, dst) in enumerate(((1, 23, 7), (-1, 8, 24))):
        side.append(pltpu.make_async_remote_copy(
            src_ref=prof.at[pl.ds(src, 1), :], dst_ref=prof.at[pl.ds(dst, 1), :],
            send_sem=side_ss.at[0, i], recv_sem=side_rs.at[0, i],
            device_id=partner(0, c), device_id_type=MESH))
        side.append(pltpu.make_async_remote_copy(
            src_ref=basis_h.at[:, pl.ds(src - 8, 1), :], dst_ref=bh.at[i],
            send_sem=side_ss.at[1, i], recv_sem=side_rs.at[1, i],
            device_id=partner(0, c), device_id_type=MESH))
    for c in far1 + first + side:
        c.start()

    def whole(ref, ss, rs):
        return pltpu.make_async_remote_copy(
            src_ref=ref, dst_ref=ref, send_sem=ss, recv_sem=rs, device_id=partner(0, 1), device_id_type=MESH)

    whole(m1r, m_ss.at[0], m_rs.at[0]).wait_recv()

    lane32 = lane_iota((32, 128))
    lane8 = lane_iota((8, 128))

    def ext_rows(own, ref, a):
        def part(c, lo, hi):
            return own[lo:hi, :] if (a, c) == (0, 0) else ref[slot_of(a, c), lo:hi, :]
        return jnp.concatenate([part(-1, 8, 16), part(0, 0, 16), part(1, 0, 8)], axis=0)

    def gather_cols(own, ref, offsets, ncols):
        cols = [jnp.zeros((32, 128), f32) for _ in range(ncols)]
        for b, a in enumerate(offsets):
            v = ext_rows(own, ref, a)
            here = (lane32 >= 16 * b) & (lane32 < 16 * b + 16)
            for i in range(ncols):
                s = (16 * (b - i)) % 128
                cols[i] = jnp.where(here, pltpu.roll(v, s, 1) if s else v, cols[i])
        return cols

    def gather_meta(offsets):
        out = jnp.zeros((8, 128), f32)
        for b, a in enumerate(offsets):
            v = m1s[16:24, :] if a == 0 else m1r[slot_of(a, 0), 16:24, :]
            here = (lane8 >= 16 * b) & (lane8 < 16 * b + 16)
            out = jnp.where(here, pltpu.roll(v, 16 * b, 1) if b else v, out)
        return out

    near_off, far_off = (-1, 0, 1), (14, 15, 16, 17, 18)
    rot_n, sta_n = gather_cols(m1s, m1r, near_off, 2)
    rot_f, sta_f = gather_cols(m1s, m1r, far_off, 2)
    meta_n, meta_f = gather_meta(near_off), gather_meta(far_off)

    drift = off_s[0] - RI
    rows = row_iota((128, 128))
    lanes = lane_iota((128, 128))

    def weights(meta, base):
        w = meta[2:3, :]
        at = lanes + (drift + base) + meta[0:1, :].astype(jnp.int32)
        return jnp.where(rows == at, 1.0 - w, 0.0) + jnp.where(rows == at + 1, w, 0.0)

    w_n = weights(meta_n, 16)
    w_f = weights(meta_f, -16)

    def opposite(rn, sn, rf, sf):
        flux = jnp.dot(sf, w_n, precision=HI, preferred_element_type=f32) - rn
        fluxf = jnp.dot(sn, w_f, precision=HI, preferred_element_type=f32) - rf
        back = lax.dot_general(fluxf, w_f, (((1,), (1,)), ((), ())), precision=HI, preferred_element_type=f32)
        return flux, back

    def local_weights(meta):
        e, w = meta[1:2, :], meta[3:4, :]
        return (1.0 - e) * (1.0 - w), (1.0 - e) * w + e * (1.0 - w), e * w

    lw_n, lw_f = local_weights(meta_n), local_weights(meta_f)

    def spread(lw, v):
        return lw[0] * right(v) + lw[1] * v + lw[2] * left(v)

    def collect(lw, v):
        return left(lw[0] * v) + lw[1] * v + right(lw[2] * v)

    bl0, bl1 = meta_n[4:5, :], meta_n[5:6, :]
    eb = spread(lw_n, bl0)
    c0 = (1.0 - 2 * DIFF) * bl0 + DIFF * (left(bl0) + right(bl0)) - ADV * (bl0 - right(bl0)) + bl1
    r32 = row_iota((32, 128))
    for i, v in enumerate((bl0, bl1, c0, collect(lw_n, bl0), collect(lw_n, eb), eb)):
        picked = jnp.where(lane32 == r32 + 15, jnp.broadcast_to(v, (32, 128)), 0.0)
        bb[i] = jnp.broadcast_to(jnp.sum(picked, axis=1, keepdims=True), (32, 128))

    def coef(i, q):
        return bb[i, pl.ds(q, 1), :]

    def wide(v):
        return jnp.concatenate([v] * 4, axis=1)

    ri = lane_iota((1, R))
    edge = (ri == RI - 1) | (ri == RI)
    ctr = jnp.where(edge, 1.0 - 5 * DIFF - ADV, 1.0 - 6 * DIFF - ADV).astype(f32)
    up = jnp.where((ri == RI - 1) | (ri == R - 1), 0.0, DIFF).astype(f32)
    dn = jnp.where((ri == RI) | (ri == 0), 0.0, DIFF).astype(f32)

    def stencil(v, strong, weak, vz):
        return ctr * v + up * left(v) + dn * right(v) + DIFF * (vz + weak) + (DIFF + ADV) * strong

    def beside(v):
        return pltpu.roll(v, 1, 0) + pltpu.roll(v, v.shape[0] - 1, 0)

    def put(ref, idx, rows_, v, flux, back, k):
        ln = lane_iota(flux.shape)
        f = jnp.where(ln == 127, pltpu.roll(flux, 127 - k, 1), 0.0)
        b = jnp.where(ln == 0, pltpu.roll(back, lax.rem(128 - k, 128), 1), 0.0)
        ref[idx, rows_, 0:128] = v[:, 0:128]
        ref[idx, rows_, 128:256] = v[:, 128:256] + DIFF * f
        ref[idx, rows_, 256:384] = v[:, 256:384] - DIFF * b
        ref[idx, rows_, 384:512] = v[:, 384:512]

    def seal(ref, n):
        @pl.when(ax == 0)
        def _():
            ref[:, pl.ds(8 - n, n), :] = jnp.zeros((ref.shape[0], n, R), f32)

        @pl.when(ax == NX - 1)
        def _():
            ref[:, pl.ds(24, n), :] = jnp.zeros((ref.shape[0], n, R), f32)

    flux0, back0 = opposite(rot_n, sta_n, rot_f, sta_f)

    for c in first + side:
        c.wait_recv()
    seal(x0, 2)
    ally = slice(0, 32)

    def step_u1(q, _):
        v = x0[q + 1]
        new = stencil(v, x0[q], x0[q + 2], beside(v)) + wide(coef(0, q)) * prof[...]
        put(u1, q, ally, new, flux0, back0, q + 15)
        return 0

    lax.fori_loop(0, 18, step_u1, 0)
    seal(u1, 1)

    def take1(q, carry):
        rot, sta = carry
        a = pltpu.roll(u1[q, 8:24, 128:256], q + 16, 1)
        b = pltpu.roll(u1[q, 8:24, 256:384], q + 15, 1)
        return jnp.where(lane == q + 15, a, rot), jnp.where(lane == q + 15, b, sta)

    rot1, sta1 = lax.fori_loop(0, 18, take1, (zero, zero))
    flux1 = spread(lw_n, sta1) - rot1
    back1 = collect(lw_n, flux1)

    centre = slice(8, 24)

    def step_u2(j, carry):
        ls, qs, ps, a1, a2, a3, cols = carry
        v = u1[j + 1]
        new = stencil(v[8:24], u1[j, 8:24, :], u1[j + 2, 8:24, :], beside(v)[8:24]) + wide(coef(1, j + 1)) * prof[8:24, :]
        put(fin, j, slice(0, 16), new, flux1, back1, j + 16)
        lam = fin[j] - tg[j]
        l2[j + 2, 8:24, :] = lam
        mid1, mid2 = lam[:, 128:256], lam[:, 256:384]
        cols = cols
        for i, (t, l) in enumerate(((mid1, 126), (mid1, 127), (mid2, 0), (mid2, 1))):
            k = j + 16 * i
            cols = jnp.where(lane == k, pltpu.roll(t, lax.rem(k + 128 - l, 128), 1), cols)
        q = j + 1
        return (ls + lam * lam, qs + wide(coef(2, q)) * lam, ps + wide(coef(0, q)) * lam,
                a1 + coef(3, q) * mid2, a2 + coef(4, q) * mid2, a3 + coef(5, q) * mid1, cols)

    big = jnp.zeros((Z, R), f32)
    ls, qs, ps, a1, a2, a3, cols = lax.fori_loop(0, J, step_u2, (big, big, big, zero, zero, zero, zero))
    m2s[...] = cols

    second = [near_copy(l2.at[plane_own[a], row_own[c], :], l2, a, c, 1) for a, c in NEAR]
    far2 = [message(m2s, m2r, a, c, 1) for a, c in PARTNERS]
    for c in far2 + second:
        c.start()

    zr = row_iota((Z, R))
    pz = jnp.where(zr == 0, 0.0, pltpu.roll(ps, 1, 0)) + jnp.where(zr == Z - 1, 0.0, pltpu.roll(ps, Z - 1, 0))
    vv = qs + (ctr - (1.0 - 6 * DIFF - ADV) - 4 * DIFF) * ps + up * left(ps) + dn * right(ps) + DIFF * pz
    at255 = jnp.where(lane == 127, left(a1) - ps[:, 128:256], 0.0)
    at256 = jnp.where(lane == 0, a2 - right(a3), 0.0)
    vv = vv + DIFF * jnp.concatenate([zero, at255, -at256, zero], axis=1)
    top = jnp.where(ax == 0, 0.0, DIFF) * ps[0:1, :]
    bot = jnp.where(ax == NX - 1, 0.0, DIFF) * ps[15:16, :]

    def fold(v):
        v = v[:, 0:128] + v[:, 128:256] + v[:, 256:384] + v[:, 384:512]
        return jnp.sum(v, axis=0, keepdims=True)

    rowsum = []
    for m in range(M):
        rowsum.append(fold(bs[m] * vv) + fold(bh[0, m] * top + bh[1, m] * bot))
    rowsum.append(fold(ls))
    rowsum.append(jnp.zeros((7, 128), f32))
    stack = jnp.concatenate(rowsum, axis=0)
    stack = jnp.broadcast_to(jnp.sum(stack, axis=1, keepdims=True), (24, 128))
    rrs[...] = jnp.sum(jnp.where(row_iota((24, 128)) == lane_iota((24, 128)), stack, 0.0), axis=0, keepdims=True)

    def tell(k, _):
        pltpu.make_async_remote_copy(
            src_ref=rrs, dst_ref=rrr.at[NA * NX - 2 - k], send_sem=rr_ss.at[0], recv_sem=rr_rs.at[0],
            device_id=ranked(k + 1), device_id_type=MESH).start()
        return 0

    lax.fori_loop(0, NA * NX - 1, tell, 0)

    whole(m2r, m_ss.at[1], m_rs.at[1]).wait_recv()
    zrow = row_iota((32, 128))
    inside = ((zrow >= 8) | (ax != 0)) & ((zrow < 24) | (ax != NX - 1))

    def adjoint_cols(cs, lw):
        c254, c255, c256, c257 = [jnp.where(inside, c, 0.0) for c in cs]
        flux = spread(lw, c256) - c255
        back = collect(lw, flux)

        def one(c, out, term):
            return (1.0 - 5 * DIFF - ADV) * c + DIFF * (out + right(c) + beside(c)) + (DIFF + ADV) * left(c) + DIFF * term

        return flux, back, one(c255, c254, flux), one(c256, c257, -back)

    flux_n, back_n, rot_n1, sta_n1 = adjoint_cols(gather_cols(m2s, m2r, near_off, 4), lw_n)
    _, _, rot_f1, sta_f1 = adjoint_cols(gather_cols(m2s, m2r, far_off, 4), lw_f)
    fluxa, backa = opposite(rot_n1[8:24], sta_n1[8:24], rot_f1[8:24], sta_f1[8:24])
    for c in second:
        c.wait_recv()
    seal(l2, 2)

    def step_l1(q, _):
        v = l2[q + 1]
        new = stencil(v, l2[q + 2], l2[q], beside(v))
        put(l1, q, ally, new, flux_n, back_n, q + 15)
        return 0

    lax.fori_loop(0, 18, step_l1, 0)
    seal(l1, 1)

    def step_l0(j, _):
        v = l1[j + 1]
        new = stencil(v[8:24], l1[j + 2, 8:24, :], l1[j, 8:24, :], beside(v)[8:24])
        put(sen, j, slice(0, 16), new, fluxa, backa, j + 16)
        return 0

    lax.fori_loop(0, J, step_l0, 0)

    whole(rrr, rr_ss.at[0], rr_rs.at[0]).wait_recv()
    total = rrs[...] + jnp.sum(rrr[...], axis=0)
    tot[...] = jnp.broadcast_to(total, (8, 128))

    for c in first + side + second:
        c.wait_send()
    whole(m1r, m_ss.at[0], m_rs.at[0]).wait_send()
    whole(m2r, m_ss.at[1], m_rs.at[1]).wait_send()
    whole(rrr, rr_ss.at[0], rr_rs.at[0]).wait_send()


def finish(fin, sen, tot, fin_o, sen_o, grad_o, loss_o, sems):
    a = pltpu.make_async_copy(fin, fin_o, sems.at[0])
    b = pltpu.make_async_copy(sen, sen_o, sems.at[1])
    a.start()
    b.start()
    row = tot[0:1, :]
    grad_o[...] = row[:, 0:M] * (1.0 / COLUMNS)
    loss_o[...] = row[:, M : M + 1] * (0.5 / (COLUMNS * R))
    a.wait()
    b.wait()


def on_device(initial, target, basis, coefficients, blade, offset, extra, frac):
    vm = pl.BlockSpec(memory_space=pltpu.VMEM)
    hbm = pl.BlockSpec(memory_space=pltpu.HBM)
    block = jax.ShapeDtypeStruct((J, Z, R), f32)
    np_ = len(PARTNERS)
    dma = pltpu.SemaphoreType.DMA
    fin, sen, tot = pl.pallas_call(
        kernel,
        out_shape=(block, block, jax.ShapeDtypeStruct((8, 128), f32)),
        in_specs=[hbm] * 8,
        out_specs=(vm, vm, vm),
        scratch_shapes=[
            pltpu.VMEM((20, 32, R), f32), pltpu.VMEM((18, 32, R), f32),
            pltpu.VMEM((20, 32, R), f32), pltpu.VMEM((18, 32, R), f32),
            pltpu.VMEM((J, Z, R), f32), pltpu.VMEM((M, Z, R), f32), pltpu.VMEM((2, M, 1, R), f32),
            pltpu.VMEM((32, R), f32),
            pltpu.VMEM((24, 128), f32), pltpu.VMEM((np_, 24, 128), f32),
            pltpu.VMEM((16, 128), f32), pltpu.VMEM((np_, 16, 128), f32),
            pltpu.VMEM((1, 128), f32), pltpu.VMEM((NA * NX - 1, 1, 128), f32),
            pltpu.VMEM((6, 32, 128), f32),
            pltpu.VMEM((2, J), f32), pltpu.VMEM((2, J), jnp.int32), pltpu.VMEM((2, J), f32),
            pltpu.SMEM((M,), f32), pltpu.SMEM((2,), jnp.int32),
            dma((8,)), dma((2, 8)), dma((2, 8)), dma((2,)), dma((2,)), dma((2, 2)), dma((2, 2)), dma((1,)), dma((1,)),
        ],
        compiler_params=pltpu.CompilerParams(collective_id=0, has_side_effects=True, vmem_limit_bytes=60 * 1024 * 1024),
    )(initial, target, basis, coefficients, blade, offset, extra, frac)
    fin, sen, grad, loss = pl.pallas_call(
        finish,
        out_shape=(block, block, jax.ShapeDtypeStruct((1, M), f32), jax.ShapeDtypeStruct((1, 1), f32)),
        in_specs=[vm] * 3,
        out_specs=(hbm, hbm, vm, vm),
        scratch_shapes=[dma((2,))],
    )(fin, sen, tot)
    return fin, sen, grad.reshape(M), loss.reshape(())


def solution(mesh):
    block = P("az", "ax", None)
    row = P(None, "az")
    return jax.shard_map(
        on_device,
        mesh=mesh,
        in_specs=(block, block, P(None, "ax", None), P(), row, P(), row, row),
        out_specs=(block, block, P(), P()),
        check_vma=False,
    )
```

time: 1080 us -> 42.9 us (0.04)
  the two profiles are of different devices: /device:TPU:0 before, /device:TPU:1 now
where the time goes in v1:
time: 42.9 us; the launch traced here: 42.8 us
  Pallas kernels  42.1 us (98%)
  between operations  0.64 us (1%)
    pallas_call x1, Pallas kernels, on_device(): pl.pallas_call(kernel, out_shape=(block, block, jax.ShapeDtypeStruct((8,...  39.4 us
    pallas_call x1, Pallas kernels, on_device(): pl.pallas_call(finish, out_shape=(block, block, jax.ShapeDtypeStruct((1,...  2.7 us

profile of v1, /device:TPU:1, one launch (start us, length us, event | category | flops | bytes accessed | tf_op | source)
XLA Modules:
  0.0 42.8 jit_solution(8517471222898337146)
XLA Ops:
  0.6 39.4 %shard_map.111 = (f32[16,16,512]{2,1,0:T(8,128)}, f32[16,16,512]{2,1,0:T(8,128)}, f32[8,128]{1,0:T(8,128)}) custom-call(f32[16,16,512]{2,1,0:T(8,128)} %u_h.1, f32[16,16,512]{2,1,0:T(8,128)} %t_h.1, f32[16,16,512]{2,1,0:T(8,128)} %basis_h.1, f32[16]{0:T(128)} %coef_h.1, f32[2,16]{1,0:T(2,128)} %blade_h.1, s32[2]{0:T(128)} %off_h.1, s32[2,16]{1,0:T(2,128)} %extra_h.1, ...), custom_call_target="tpu_custom_call" | custom-call | tf_op jit(solution)/shard_map/pallas_call | solution.py:406
  40.1 2.7 %shard_map.112 = (f32[16,16,512]{2,1,0:T(8,128)}, f32[16,16,512]{2,1,0:T(8,128)}, f32[1,16]{1,0:T(1,128)}, f32[1,1]{1,0:T(1,128)}) custom-call(f32[16,16,512]{2,1,0:T(8,128)} %get-tuple-element.11.fin, f32[16,16,512]{2,1,0:T(8,128)} %get-tuple-element.12.sen, f32[8,128]{1,0:T(8,128)} %get-tuple-element.13.tot), custom_call_target="tpu_custom_call" | custom-call | tf_op jit(solution)/shard_map/pallas_call | solution.py:426

commit v2 on v1

--- a/solution.py
+++ b/solution.py
@@ -19,11 +19,17 @@
 
 NEAR = [(a, c) for a in (-1, 0, 1) for c in (-1, 0, 1) if (a, c) != (0, 0)]
 FAR = [(a, c) for a in (14, 15, 16, 17, 18) for c in (-1, 0, 1)]
-PARTNERS = FAR + NEAR
+GROUPS = (0, 1, -1)
+PARTNERS = {g: [(a, c) for a, c in FAR + NEAR if c == g] for g in GROUPS}
+GREETED = FAR + NEAR + [(6, 0), (6, 2), (-6, 0), (-6, 2)]
+OTHERS = sorted(
+    [(x, y, z, c) for x in range(4) for y in range(4) for z in range(4) for c in range(2) if x + y + z + c],
+    key=lambda o: -(sum(v > 0 for v in o[:3]) * 8 + sum(v == 2 for v in o[:3])),
+)
 
 
 def slot_of(a, c):
-    return [((x + 8) % NA, y) for x, y in PARTNERS].index(((a + 8) % NA, c))
+    return [x % NA for x, _ in PARTNERS[c]].index(a % NA)
 
 
 def lane_iota(shape):
@@ -45,65 +51,62 @@
 def kernel(
     u_h, t_h, basis_h, coef_h, blade_h, off_h, extra_h, frac_h,
     fin, sen, tot,
-    x0, u1, l2, l1, tg, bs, bh, prof, m1s, m1r, m2s, m2r, rrs, rrr, bb,
+    x0, u1, l2, l1, tg, bs, bh, prof, m1s, m1r0, m1rp, m1rm, m2s, m2r0, m2rp, m2rm, rrs, rrr, bb,
     blade_v, extra_v, frac_v, coef_s, off_s,
-    loc, near_ss, near_rs, m_ss, m_rs, side_ss, side_rs, rr_ss, rr_rs,
+    loc, near_ss, near_rs, m_ss, m_rs, side_ss, side_rs, rr_ss, rr_rs, ready,
 ):
     az, ax = lax.axis_index("az"), lax.axis_index("ax")
-    me = az * NX + ax
 
     def partner(a, c):
-        return (lax.rem(az + a + NA, NA), lax.rem(ax + c + NX, NX))
-
-    def ranked(k):
-        t = lax.rem(me + k, NA * NX)
-        return (t // NX, lax.rem(t, NX))
-
-    barrier = pltpu.get_barrier_semaphore()
-
-    def greet(k, _):
-        pl.semaphore_signal(barrier, inc=1, device_id=ranked(k + 1), device_id_type=MESH)
-        return 0
-
-    lax.fori_loop(0, NA * NX - 1, greet, 0)
+        return ((az + a) & (NA - 1), (ax + c) & (NX - 1))
+
+    def guard(c, act):
+        if c == 0:
+            act()
+        else:
+            pl.when((ax < NX - 1) if c > 0 else (ax > 0))(act)
 
     loads = [
         pltpu.make_async_copy(u_h, x0.at[2:18, 8:24, :], loc.at[0]),
-        pltpu.make_async_copy(basis_h, bs, loc.at[1]),
-        pltpu.make_async_copy(coef_h, coef_s, loc.at[2]),
-        pltpu.make_async_copy(off_h, off_s, loc.at[3]),
-        pltpu.make_async_copy(blade_h, blade_v, loc.at[4]),
-        pltpu.make_async_copy(extra_h, extra_v, loc.at[5]),
-        pltpu.make_async_copy(frac_h, frac_v, loc.at[6]),
+        pltpu.make_async_copy(blade_h, blade_v, loc.at[1]),
+        pltpu.make_async_copy(extra_h, extra_v, loc.at[2]),
+        pltpu.make_async_copy(frac_h, frac_v, loc.at[3]),
+        pltpu.make_async_copy(coef_h, coef_s, loc.at[4]),
+        pltpu.make_async_copy(off_h, off_s, loc.at[5]),
+        pltpu.make_async_copy(basis_h, bs, loc.at[6]),
         pltpu.make_async_copy(t_h, tg, loc.at[7]),
     ]
     for c in loads:
         c.start()
 
-    m1s[...] = jnp.zeros((24, 128), f32)
-    for c in loads:
+    barrier = pltpu.get_barrier_semaphore()
+
+    for a, c in GREETED:
+        pl.semaphore_signal(barrier, inc=1, device_id=partner(a, c), device_id_type=MESH)
+
+    loads[0].wait()
+    tile = (8, 128)
+    lane8 = lane_iota(tile)
+
+    def take(j, acc):
+        for i, (lo, k) in enumerate(((128, 1), (256, 0))):
+            for h in range(2):
+                at = 16 + 16 * i + 32 * h + j
+                acc = jnp.where(lane8 == at, pltpu.roll(x0[j + 2, 8 + 8 * h : 16 + 8 * h, lo : lo + 128], lax.rem(at + k, 128), 1), acc)
+        return acc
+
+    taken = lax.fori_loop(0, J, take, jnp.zeros(tile, f32), unroll=True)
+    for c in loads[1:4]:
         c.wait()
-    lane = lane_iota((Z, 128))
-
-    def take(j, carry):
-        rot, sta = carry
-        a = pltpu.roll(x0[j + 2, 8:24, 128:256], j + 1, 1)
-        b = pltpu.roll(x0[j + 2, 8:24, 256:384], j + 16, 1)
-        return jnp.where(lane == j, a, rot), jnp.where(lane == j + 16, b, sta)
-
-    zero = jnp.zeros((Z, 128), f32)
-    rot, sta = lax.fori_loop(0, J, take, (zero, zero))
-    m1s[0:16, :] = rot + sta
-    m1s[16:18, 0:16] = extra_v[...].astype(f32)
-    m1s[18:20, 0:16] = frac_v[...]
-    m1s[20:22, 0:16] = blade_v[...]
-
-    def mix(m, acc):
-        return acc + coef_s[m] * bs[m]
-
-    prof[8:24, :] = lax.fori_loop(0, M, mix, jnp.zeros((Z, R), f32))
-
-    pl.semaphore_wait(barrier, NA * NX - 1)
+    m1s[...] = jnp.zeros(tile, f32)
+    m1s[0:2, 0:16] = extra_v[...].astype(f32)
+    m1s[2:4, 0:16] = frac_v[...]
+    m1s[4:6, 0:16] = blade_v[...]
+    m1s[...] = m1s[...] + taken
+
+    pl.semaphore_wait(barrier, len(GREETED))
+    for a, c in GREETED:
+        pl.semaphore_signal(ready, inc=1, device_id=partner(a, c), device_id_type=MESH)
 
     plane_src = {-1: pl.ds(0, 2), 0: pl.ds(0, 16), 1: pl.ds(14, 2)}
     row_src = {-1: pl.ds(0, 2), 0: pl.ds(0, 16), 1: pl.ds(14, 2)}
@@ -122,61 +125,115 @@
 
     def message(src, dst, a, c, n):
         return pltpu.make_async_remote_copy(
-            src_ref=src, dst_ref=dst.at[slot_of(-a, -c)],
-            send_sem=m_ss.at[n], recv_sem=m_rs.at[n],
+            src_ref=src, dst_ref=dst[-c].at[slot_of(-a, -c)],
+            send_sem=m_ss.at[n, c + 1], recv_sem=m_rs.at[n, 1 - c],
             device_id=partner(a, c), device_id_type=MESH,
         )
 
-    first = [near_copy(u_h.at[plane_src[a], row_src[c], :], x0, a, c, 0) for a, c in NEAR]
-    far1 = [message(m1s, m1r, a, c, 0) for a, c in PARTNERS]
-    side = []
-    for i, (c, src, dst) in enumerate(((1, 23, 7), (-1, 8, 24))):
-        side.append(pltpu.make_async_remote_copy(
-            src_ref=prof.at[pl.ds(src, 1), :], dst_ref=prof.at[pl.ds(dst, 1), :],
-            send_sem=side_ss.at[0, i], recv_sem=side_rs.at[0, i],
-            device_id=partner(0, c), device_id_type=MESH))
-        side.append(pltpu.make_async_remote_copy(
-            src_ref=basis_h.at[:, pl.ds(src - 8, 1), :], dst_ref=bh.at[i],
-            send_sem=side_ss.at[1, i], recv_sem=side_rs.at[1, i],
-            device_id=partner(0, c), device_id_type=MESH))
-    for c in far1 + first + side:
-        c.start()
+    def near_group(c):
+        return sorted((n for n in NEAR if n[1] == c), key=lambda n: -abs(n[0]))
+
+    def send_all(near_of, src, dst, n, c):
+        def act():
+            for a, _ in near_group(c):
+                near_of(a, c).start()
+            for a, _ in PARTNERS[c]:
+                message(src, dst, a, c, n).start()
+        guard(c, act)
+
+    m1g = {0: m1r0, 1: m1rp, -1: m1rm}
+    m2g = {0: m2r0, 1: m2rp, -1: m2rm}
+
+    def near1(a, c):
+        return near_copy(u_h.at[plane_src[a], row_src[c], :], x0, a, c, 0)
+
+    for c in GROUPS:
+        send_all(near1, m1s, m1g, 0, c)
+
+    for c in loads[4:]:
+        c.wait()
+
+    def mix(m, acc):
+        return acc + coef_s[m] * bs[m]
+
+    prof[8:24, :] = lax.fori_loop(0, M, mix, jnp.zeros((Z, R), f32), unroll=4)
+
+    def side(c):
+        i, src, dst = (0, 23, 7) if c > 0 else (1, 8, 24)
+        return (
+            pltpu.make_async_remote_copy(
+                src_ref=prof.at[pl.ds(src, 1), :], dst_ref=prof.at[pl.ds(dst, 1), :],
+                send_sem=side_ss.at[0, i], recv_sem=side_rs.at[0, i],
+                device_id=partner(0, c), device_id_type=MESH),
+            pltpu.make_async_remote_copy(
+                src_ref=basis_h.at[:, pl.ds(src - 8, 1), :], dst_ref=bh.at[i],
+                send_sem=side_ss.at[1, i], recv_sem=side_rs.at[1, i],
+                device_id=partner(0, c), device_id_type=MESH),
+        )
+
+    for c in (1, -1):
+        def act(c=c):
+            for copy in side(c):
+                copy.start()
+        guard(c, act)
 
     def whole(ref, ss, rs):
         return pltpu.make_async_remote_copy(
             src_ref=ref, dst_ref=ref, send_sem=ss, recv_sem=rs, device_id=partner(0, 1), device_id_type=MESH)
 
-    whole(m1r, m_ss.at[0], m_rs.at[0]).wait_recv()
+    def arrivals(dst, n):
+        for c in GROUPS:
+            guard(c, lambda c=c: whole(dst[c], m_ss.at[n, c + 1], m_rs.at[n, c + 1]).wait_recv())
+
+    def departures(dst, n):
+        for c in GROUPS:
+            guard(c, lambda c=c: whole(dst[c], m_ss.at[n, c + 1], m_rs.at[n, c + 1]).wait_send())
+
+    def near_arrivals(near_of):
+        for c in GROUPS:
+            def act(c=c):
+                for a, _ in near_group(c):
+                    near_of(-a, -c).wait_recv()
+            guard(c, act)
+
+    def near_departures(near_of):
+        for c in GROUPS:
+            def act(c=c):
+                for a, _ in near_group(c):
+                    near_of(a, c).wait_send()
+            guard(c, act)
+
+    arrivals(m1g, 0)
 
     lane32 = lane_iota((32, 128))
-    lane8 = lane_iota((8, 128))
-
-    def ext_rows(own, ref, a):
-        def part(c, lo, hi):
-            return own[lo:hi, :] if (a, c) == (0, 0) else ref[slot_of(a, c), lo:hi, :]
-        return jnp.concatenate([part(-1, 8, 16), part(0, 0, 16), part(1, 0, 8)], axis=0)
-
-    def gather_cols(own, ref, offsets, ncols):
-        cols = [jnp.zeros((32, 128), f32) for _ in range(ncols)]
-        for b, a in enumerate(offsets):
-            v = ext_rows(own, ref, a)
-            here = (lane32 >= 16 * b) & (lane32 < 16 * b + 16)
-            for i in range(ncols):
-                s = (16 * (b - i)) % 128
-                cols[i] = jnp.where(here, pltpu.roll(v, s, 1) if s else v, cols[i])
+
+    def gather_cols(own, ref, offsets, bases):
+        def part(c, a, base, b):
+            v = own[...] if (a, c) == (0, 0) else ref[c][slot_of(a, c)]
+            s = (16 * b - base) % 128
+            return pltpu.roll(v, s, 1) if s else v
+
+        cols = []
+        for lo, hi in bases:
+            out = jnp.zeros((32, 128), f32)
+            for b, a in enumerate(offsets):
+                v = jnp.concatenate([part(-1, a, hi, b), part(0, a, lo, b), part(0, a, hi, b), part(1, a, lo, b)], axis=0)
+                out = jnp.where((lane32 >= 16 * b) & (lane32 < 16 * b + 16), v, out)
+            cols.append(out)
         return cols
 
     def gather_meta(offsets):
         out = jnp.zeros((8, 128), f32)
         for b, a in enumerate(offsets):
-            v = m1s[16:24, :] if a == 0 else m1r[slot_of(a, 0), 16:24, :]
-            here = (lane8 >= 16 * b) & (lane8 < 16 * b + 16)
-            out = jnp.where(here, pltpu.roll(v, 16 * b, 1) if b else v, out)
+            v = m1s[...] if a == 0 else m1g[0][slot_of(a, 0)]
+            out = jnp.where((lane8 >= 16 * b) & (lane8 < 16 * b + 16), pltpu.roll(v, 16 * b, 1) if b else v, out)
         return out
 
+    bases1 = ((16, 48), (32, 64))
+    bases2 = ((0, 64), (16, 80), (32, 96), (48, 112))
     near_off, far_off = (-1, 0, 1), (14, 15, 16, 17, 18)
-    rot_n, sta_n = gather_cols(m1s, m1r, near_off, 2)
-    rot_f, sta_f = gather_cols(m1s, m1r, far_off, 2)
+    rot_n, sta_n = gather_cols(m1s, m1g, near_off, bases1)
+    rot_f, sta_f = gather_cols(m1s, m1g, far_off, bases1)
     meta_n, meta_f = gather_meta(near_off), gather_meta(far_off)
 
     drift = off_s[0] - RI
@@ -255,8 +312,12 @@
 
     flux0, back0 = opposite(rot_n, sta_n, rot_f, sta_f)
 
-    for c in first + side:
-        c.wait_recv()
+    near_arrivals(near1)
+    for c in (1, -1):
+        def act(c=c):
+            for copy in side(-c):
+                copy.wait_recv()
+        guard(c, act)
     seal(x0, 2)
     ally = slice(0, 32)
 
@@ -266,7 +327,7 @@
         put(u1, q, ally, new, flux0, back0, q + 15)
         return 0
 
-    lax.fori_loop(0, 18, step_u1, 0)
+    lax.fori_loop(0, 18, step_u1, 0, unroll=3)
     seal(u1, 1)
 
     def take1(q, carry):
@@ -275,7 +336,9 @@
         b = pltpu.roll(u1[q, 8:24, 256:384], q + 15, 1)
         return jnp.where(lane == q + 15, a, rot), jnp.where(lane == q + 15, b, sta)
 
-    rot1, sta1 = lax.fori_loop(0, 18, take1, (zero, zero))
+    lane = lane_iota((Z, 128))
+    zero = jnp.zeros((Z, 128), f32)
+    rot1, sta1 = lax.fori_loop(0, 18, take1, (zero, zero), unroll=18)
     flux1 = spread(lw_n, sta1) - rot1
     back1 = collect(lw_n, flux1)
 
@@ -289,22 +352,23 @@
         lam = fin[j] - tg[j]
         l2[j + 2, 8:24, :] = lam
         mid1, mid2 = lam[:, 128:256], lam[:, 256:384]
-        cols = cols
         for i, (t, l) in enumerate(((mid1, 126), (mid1, 127), (mid2, 0), (mid2, 1))):
-            k = j + 16 * i
-            cols = jnp.where(lane == k, pltpu.roll(t, lax.rem(k + 128 - l, 128), 1), cols)
+            for h in range(2):
+                k = j + bases2[i][h]
+                cols = jnp.where(lane8 == k, pltpu.roll(t[8 * h : 8 * h + 8], lax.rem(k + 128 - l, 128), 1), cols)
         q = j + 1
         return (ls + lam * lam, qs + wide(coef(2, q)) * lam, ps + wide(coef(0, q)) * lam,
                 a1 + coef(3, q) * mid2, a2 + coef(4, q) * mid2, a3 + coef(5, q) * mid1, cols)
 
     big = jnp.zeros((Z, R), f32)
-    ls, qs, ps, a1, a2, a3, cols = lax.fori_loop(0, J, step_u2, (big, big, big, zero, zero, zero, zero))
+    ls, qs, ps, a1, a2, a3, cols = lax.fori_loop(0, J, step_u2, (big, big, big, zero, zero, zero, jnp.zeros(tile, f32)), unroll=2)
     m2s[...] = cols
 
-    second = [near_copy(l2.at[plane_own[a], row_own[c], :], l2, a, c, 1) for a, c in NEAR]
-    far2 = [message(m2s, m2r, a, c, 1) for a, c in PARTNERS]
-    for c in far2 + second:
-        c.start()
+    def near2(a, c):
+        return near_copy(l2.at[plane_own[a], row_own[c], :], l2, a, c, 1)
+
+    for c in GROUPS:
+        send_all(near2, m2s, m2g, 1, c)
 
     zr = row_iota((Z, R))
     pz = jnp.where(zr == 0, 0.0, pltpu.roll(ps, 1, 0)) + jnp.where(zr == Z - 1, 0.0, pltpu.roll(ps, Z - 1, 0))
@@ -328,15 +392,18 @@
     stack = jnp.broadcast_to(jnp.sum(stack, axis=1, keepdims=True), (24, 128))
     rrs[...] = jnp.sum(jnp.where(row_iota((24, 128)) == lane_iota((24, 128)), stack, 0.0), axis=0, keepdims=True)
 
-    def tell(k, _):
+    pl.semaphore_wait(ready, len(GREETED))
+    px, pz_, py, pc = (az >> 2) & 3, az & 3, (ax >> 1) * 2 + (az >> 4), ax & 1
+    xs = [((px + d) & 3) << 2 for d in range(4)]
+    zs = [(pz_ + d) & 3 for d in range(4)]
+    ys = [(((py + d) & 1) << 4, (((py + d) >> 1) & 1) << 1) for d in range(4)]
+    cs = [pc, 1 - pc]
+    for x, y, z, c in OTHERS:
         pltpu.make_async_remote_copy(
-            src_ref=rrs, dst_ref=rrr.at[NA * NX - 2 - k], send_sem=rr_ss.at[0], recv_sem=rr_rs.at[0],
-            device_id=ranked(k + 1), device_id_type=MESH).start()
-        return 0
-
-    lax.fori_loop(0, NA * NX - 1, tell, 0)
-
-    whole(m2r, m_ss.at[1], m_rs.at[1]).wait_recv()
+            src_ref=rrs, dst_ref=rrr.at[OTHERS.index((-x % 4, -y % 4, -z % 4, c))], send_sem=rr_ss.at[0], recv_sem=rr_rs.at[0],
+            device_id=(ys[y][0] + xs[x] + zs[z], ys[y][1] + cs[c]), device_id_type=MESH).start()
+
+    arrivals(m2g, 1)
     zrow = row_iota((32, 128))
     inside = ((zrow >= 8) | (ax != 0)) & ((zrow < 24) | (ax != NX - 1))
 
@@ -350,11 +417,10 @@
 
         return flux, back, one(c255, c254, flux), one(c256, c257, -back)
 
-    flux_n, back_n, rot_n1, sta_n1 = adjoint_cols(gather_cols(m2s, m2r, near_off, 4), lw_n)
-    _, _, rot_f1, sta_f1 = adjoint_cols(gather_cols(m2s, m2r, far_off, 4), lw_f)
+    flux_n, back_n, rot_n1, sta_n1 = adjoint_cols(gather_cols(m2s, m2g, near_off, bases2), lw_n)
+    _, _, rot_f1, sta_f1 = adjoint_cols(gather_cols(m2s, m2g, far_off, bases2), lw_f)
     fluxa, backa = opposite(rot_n1[8:24], sta_n1[8:24], rot_f1[8:24], sta_f1[8:24])
-    for c in second:
-        c.wait_recv()
+    near_arrivals(near2)
     seal(l2, 2)
 
     def step_l1(q, _):
@@ -363,7 +429,7 @@
         put(l1, q, ally, new, flux_n, back_n, q + 15)
         return 0
 
-    lax.fori_loop(0, 18, step_l1, 0)
+    lax.fori_loop(0, 18, step_l1, 0, unroll=3)
     seal(l1, 1)
 
     def step_l0(j, _):
@@ -372,16 +438,21 @@
         put(sen, j, slice(0, 16), new, fluxa, backa, j + 16)
         return 0
 
-    lax.fori_loop(0, J, step_l0, 0)
+    lax.fori_loop(0, J, step_l0, 0, unroll=4)
 
     whole(rrr, rr_ss.at[0], rr_rs.at[0]).wait_recv()
     total = rrs[...] + jnp.sum(rrr[...], axis=0)
     tot[...] = jnp.broadcast_to(total, (8, 128))
 
-    for c in first + side + second:
-        c.wait_send()
-    whole(m1r, m_ss.at[0], m_rs.at[0]).wait_send()
-    whole(m2r, m_ss.at[1], m_rs.at[1]).wait_send()
+    near_departures(near1)
+    near_departures(near2)
+    departures(m1g, 0)
+    departures(m2g, 1)
+    for c in (1, -1):
+        def act(c=c):
+            for copy in side(c):
+                copy.wait_send()
+        guard(c, act)
     whole(rrr, rr_ss.at[0], rr_rs.at[0]).wait_send()
 
 
@@ -401,11 +472,10 @@
     vm = pl.BlockSpec(memory_space=pltpu.VMEM)
     hbm = pl.BlockSpec(memory_space=pltpu.HBM)
     block = jax.ShapeDtypeStruct((J, Z, R), f32)
-    np_ = len(PARTNERS)
     dma = pltpu.SemaphoreType.DMA
     fin, sen, tot = pl.pallas_call(
         kernel,
-        out_shape=(block, block, jax.ShapeDtypeStruct((8, 128), f32)),
+        out_shape=(pltpu.VMEM((J, Z, R), f32), pltpu.VMEM((J, Z, R), f32), pltpu.VMEM((8, 128), f32)),
         in_specs=[hbm] * 8,
         out_specs=(vm, vm, vm),
         scratch_shapes=[
@@ -413,23 +483,23 @@
             pltpu.VMEM((20, 32, R), f32), pltpu.VMEM((18, 32, R), f32),
             pltpu.VMEM((J, Z, R), f32), pltpu.VMEM((M, Z, R), f32), pltpu.VMEM((2, M, 1, R), f32),
             pltpu.VMEM((32, R), f32),
-            pltpu.VMEM((24, 128), f32), pltpu.VMEM((np_, 24, 128), f32),
-            pltpu.VMEM((16, 128), f32), pltpu.VMEM((np_, 16, 128), f32),
+            *[pltpu.VMEM((8, 128), f32), *[pltpu.VMEM((len(PARTNERS[c]), 8, 128), f32) for c in GROUPS]] * 2,
             pltpu.VMEM((1, 128), f32), pltpu.VMEM((NA * NX - 1, 1, 128), f32),
             pltpu.VMEM((6, 32, 128), f32),
             pltpu.VMEM((2, J), f32), pltpu.VMEM((2, J), jnp.int32), pltpu.VMEM((2, J), f32),
             pltpu.SMEM((M,), f32), pltpu.SMEM((2,), jnp.int32),
-            dma((8,)), dma((2, 8)), dma((2, 8)), dma((2,)), dma((2,)), dma((2, 2)), dma((2, 2)), dma((1,)), dma((1,)),
+            dma((8,)), dma((2, 8)), dma((2, 8)), dma((2, 3)), dma((2, 3)), dma((2, 2)), dma((2, 2)), dma((1,)), dma((1,)),
+            pltpu.SemaphoreType.REGULAR,
         ],
-        compiler_params=pltpu.CompilerParams(collective_id=0, has_side_effects=True, vmem_limit_bytes=60 * 1024 * 1024),
-    )(initial, target, basis, coefficients, blade, offset, extra, frac)
+        compiler_params=pltpu.CompilerParams(collective_id=0, has_side_effects=True, vmem_limit_bytes=40 * 1024 * 1024),
+    )(*(pltpu.with_memory_space_constraint(v, pltpu.HBM) for v in (initial, target, basis, coefficients, blade, offset, extra, frac)))
     fin, sen, grad, loss = pl.pallas_call(
         finish,
         out_shape=(block, block, jax.ShapeDtypeStruct((1, M), f32), jax.ShapeDtypeStruct((1, 1), f32)),
         in_specs=[vm] * 3,
         out_specs=(hbm, hbm, vm, vm),
         scratch_shapes=[dma((2,))],
-    )(fin, sen, tot)
+    )(*(pltpu.with_memory_space_constraint(v, pltpu.VMEM) for v in (fin, sen, tot)))
     return fin, sen, grad.reshape(M), loss.reshape(())
 
 

time: 42.9 us -> 33.2 us (0.77)
  Pallas kernels: 42.1 us -> 32.4 us
    pallas_call x1, Pallas kernels: 39.4 us -> 30.9 us  [on_device(): pl.pallas_call(kernel, out_shape=(pltpu.VMEM((J, Z, R), f32), pltpu.VMEM(...]
    pallas_call x1, Pallas kernels: 2.7 us -> 1.5 us  [on_device(): pl.pallas_call(finish, out_shape=(block, block, jax.ShapeDtypeStruct((1,...]
where the time goes in v2:
time: 33.2 us; the launch traced here: 33 us
  Pallas kernels  32.4 us (98%)
  between operations  0.64 us (2%)
    pallas_call x1, Pallas kernels, on_device(): pl.pallas_call(kernel, out_shape=(pltpu.VMEM((J, Z, R), f32), pltpu.VMEM(...  30.9 us
    pallas_call x1, Pallas kernels, on_device(): pl.pallas_call(finish, out_shape=(block, block, jax.ShapeDtypeStruct((1,...  1.5 us

profile of v2, /device:TPU:1, one launch (start us, length us, event | category | flops | bytes accessed | tf_op | source)
XLA Modules:
  0.0 33.0 jit_solution(9072396655775817096)
XLA Ops:
  0.6 30.9 %shard_map.111 = (f32[16,16,512]{2,1,0:T(8,128)S(1)}, f32[16,16,512]{2,1,0:T(8,128)S(1)}, f32[8,128]{1,0:T(8,128)S(1)}) custom-call(f32[16,16,512]{2,1,0:T(8,128)} %u_h.1, f32[16,16,512]{2,1,0:T(8,128)} %t_h.1, f32[16,16,512]{2,1,0:T(8,128)} %basis_h.1, f32[16]{0:T(128)} %coef_h.1, f32[2,16]{1,0:T(2,128)} %blade_h.1, s32[2]{0:T(128)} %off_h.1, ...), custom_call_target="tpu_custom_call" | custom-call | tf_op jit(solution)/shard_map/pallas_call | solution.py:476
  31.5 1.5 %shard_map.112 = (f32[16,16,512]{2,1,0:T(8,128)}, f32[16,16,512]{2,1,0:T(8,128)}, f32[1,16]{1,0:T(1,128)}, f32[1,1]{1,0:T(1,128)}) custom-call(f32[16,16,512]{2,1,0:T(8,128)S(1)} %get-tuple-element.11.fin, f32[16,16,512]{2,1,0:T(8,128)S(1)} %get-tuple-element.12.sen, f32[8,128]{1,0:T(8,128)S(1)} %get-tuple-element.13.tot), custom_call_target="tpu_custom_call" | custom-call | tf_op jit(solution)/shard_map/pallas_call | solution.py:496

commit v3 on v2

--- a/solution.py
+++ b/solution.py
@@ -20,8 +20,12 @@
 NEAR = [(a, c) for a in (-1, 0, 1) for c in (-1, 0, 1) if (a, c) != (0, 0)]
 FAR = [(a, c) for a in (14, 15, 16, 17, 18) for c in (-1, 0, 1)]
 GROUPS = (0, 1, -1)
-PARTNERS = {g: [(a, c) for a, c in FAR + NEAR if c == g] for g in GROUPS}
-GREETED = FAR + NEAR + [(6, 0), (6, 2), (-6, 0), (-6, 2)]
+LATE, SAME, OPPOSITE = range(3)
+PARTNERS = {
+    (k, g): [(a, c) for a, c in NEAR + FAR if c == g and k == (OPPOSITE if a > 1 else LATE if a else SAME)]
+    for k in range(3) for g in GROUPS if (k, g) != (SAME, 0)
+}
+GREETED = NEAR + FAR + [(6, 0), (6, 2), (-6, 0), (-6, 2)]
 OTHERS = sorted(
     [(x, y, z, c) for x in range(4) for y in range(4) for z in range(4) for c in range(2) if x + y + z + c],
     key=lambda o: -(sum(v > 0 for v in o[:3]) * 8 + sum(v == 2 for v in o[:3])),
@@ -29,7 +33,8 @@
 
 
 def slot_of(a, c):
-    return [x % NA for x, _ in PARTNERS[c]].index(a % NA)
+    k = OPPOSITE if 1 < a % NA < NA - 1 else LATE if a else SAME
+    return k, [x % NA for x, _ in PARTNERS[k, c]].index(a % NA)
 
 
 def lane_iota(shape):
@@ -51,7 +56,7 @@
 def kernel(
     u_h, t_h, basis_h, coef_h, blade_h, off_h, extra_h, frac_h,
     fin, sen, tot,
-    x0, u1, l2, l1, tg, bs, bh, prof, m1s, m1r0, m1rp, m1rm, m2s, m2r0, m2rp, m2rm, rrs, rrr, bb,
+    x0, u1, l2, l1, tg, bs, bh, prof, m1s, m1r, m2s, m2r, rrs, rrr, bb,
     blade_v, extra_v, frac_v, coef_s, off_s,
     loc, near_ss, near_rs, m_ss, m_rs, side_ss, side_rs, rr_ss, rr_rs, ready,
 ):
@@ -76,13 +81,13 @@
         pltpu.make_async_copy(basis_h, bs, loc.at[6]),
         pltpu.make_async_copy(t_h, tg, loc.at[7]),
     ]
-    for c in loads:
-        c.start()
-
+    loads[0].start()
     barrier = pltpu.get_barrier_semaphore()
 
     for a, c in GREETED:
         pl.semaphore_signal(barrier, inc=1, device_id=partner(a, c), device_id_type=MESH)
+    for c in loads[1:]:
+        c.start()
 
     loads[0].wait()
     tile = (8, 128)
@@ -105,9 +110,6 @@
     m1s[...] = m1s[...] + taken
 
     pl.semaphore_wait(barrier, len(GREETED))
-    for a, c in GREETED:
-        pl.semaphore_signal(ready, inc=1, device_id=partner(a, c), device_id_type=MESH)
-
     plane_src = {-1: pl.ds(0, 2), 0: pl.ds(0, 16), 1: pl.ds(14, 2)}
     row_src = {-1: pl.ds(0, 2), 0: pl.ds(0, 16), 1: pl.ds(14, 2)}
     plane_dst = {-1: pl.ds(18, 2), 0: pl.ds(2, 16), 1: pl.ds(0, 2)}
@@ -124,31 +126,36 @@
         )
 
     def message(src, dst, a, c, n):
+        k, i = slot_of(-a, -c)
         return pltpu.make_async_remote_copy(
-            src_ref=src, dst_ref=dst[-c].at[slot_of(-a, -c)],
-            send_sem=m_ss.at[n, c + 1], recv_sem=m_rs.at[n, 1 - c],
+            src_ref=src, dst_ref=dst[k, -c].at[i],
+            send_sem=m_ss.at[n, k, c + 1], recv_sem=m_rs.at[n, k, 1 - c],
             device_id=partner(a, c), device_id_type=MESH,
         )
 
-    def near_group(c):
-        return sorted((n for n in NEAR if n[1] == c), key=lambda n: -abs(n[0]))
-
-    def send_all(near_of, src, dst, n, c):
-        def act():
-            for a, _ in near_group(c):
-                near_of(a, c).start()
-            for a, _ in PARTNERS[c]:
-                message(src, dst, a, c, n).start()
-        guard(c, act)
-
-    m1g = {0: m1r0, 1: m1rp, -1: m1rm}
-    m2g = {0: m2r0, 1: m2rp, -1: m2rm}
+    def near_group(k, c):
+        return [n for n in NEAR if n[1] == c and (k == LATE) == (n[0] != 0)] if k != OPPOSITE else []
+
+    def send_all(near_of, src, dst, n):
+        for c in GROUPS:
+            def act(c=c):
+                for k in range(3):
+                    for a, _ in near_group(k, c):
+                        near_of(a, c).start()
+                    for a, _ in PARTNERS.get((k, c), ()):
+                        message(src, dst, a, c, n).start()
+            guard(c, act)
+
+    m1g = dict(zip(PARTNERS, m1r))
+    m2g = dict(zip(PARTNERS, m2r))
 
     def near1(a, c):
         return near_copy(u_h.at[plane_src[a], row_src[c], :], x0, a, c, 0)
 
-    for c in GROUPS:
-        send_all(near1, m1s, m1g, 0, c)
+    send_all(near1, m1s, m1g, 0)
+
+    for a, c in GREETED:
+        pl.semaphore_signal(ready, inc=1, device_id=partner(a, c), device_id_type=MESH)
 
     for c in loads[4:]:
         c.wait()
@@ -181,35 +188,39 @@
         return pltpu.make_async_remote_copy(
             src_ref=ref, dst_ref=ref, send_sem=ss, recv_sem=rs, device_id=partner(0, 1), device_id_type=MESH)
 
-    def arrivals(dst, n):
-        for c in GROUPS:
-            guard(c, lambda c=c: whole(dst[c], m_ss.at[n, c + 1], m_rs.at[n, c + 1]).wait_recv())
-
-    def departures(dst, n):
-        for c in GROUPS:
-            guard(c, lambda c=c: whole(dst[c], m_ss.at[n, c + 1], m_rs.at[n, c + 1]).wait_send())
-
-    def near_arrivals(near_of):
+    def arrivals(near_of, dst, n, k):
         for c in GROUPS:
             def act(c=c):
-                for a, _ in near_group(c):
+                if (k, c) in PARTNERS:
+                    whole(dst[k, c], m_ss.at[n, k, c + 1], m_rs.at[n, k, c + 1]).wait_recv()
+                for a, _ in near_group(k, c):
                     near_of(-a, -c).wait_recv()
             guard(c, act)
 
-    def near_departures(near_of):
+    def departures(near_of, dst, n):
         for c in GROUPS:
             def act(c=c):
-                for a, _ in near_group(c):
-                    near_of(a, c).wait_send()
+                for k in range(3):
+                    if (k, c) in PARTNERS:
+                        whole(dst[k, c], m_ss.at[n, k, c + 1], m_rs.at[n, k, c + 1]).wait_send()
+                    for a, _ in near_group(k, c):
+                        near_of(a, c).wait_send()
             guard(c, act)
 
-    arrivals(m1g, 0)
-
+    arrivals(near1, m1g, 0, SAME)
+    for c in (1, -1):
+        def act(c=c):
+            for copy in side(-c):
+                copy.wait_recv()
+        guard(c, act)
     lane32 = lane_iota((32, 128))
 
-    def gather_cols(own, ref, offsets, bases):
+    near_off, far_off = (-1, 0, 1), (14, 15, 16, 17, 18)
+
+    def gather_cols(own, ref, offsets, only, bases):
         def part(c, a, base, b):
-            v = own[...] if (a, c) == (0, 0) else ref[c][slot_of(a, c)]
+            k, i = slot_of(a, c) if (a, c) != (0, 0) else (0, 0)
+            v = own[...] if (a, c) == (0, 0) else ref[k, c][i]
             s = (16 * b - base) % 128
             return pltpu.roll(v, s, 1) if s else v
 
@@ -217,25 +228,25 @@
         for lo, hi in bases:
             out = jnp.zeros((32, 128), f32)
             for b, a in enumerate(offsets):
+                if a not in only:
+                    continue
                 v = jnp.concatenate([part(-1, a, hi, b), part(0, a, lo, b), part(0, a, hi, b), part(1, a, lo, b)], axis=0)
                 out = jnp.where((lane32 >= 16 * b) & (lane32 < 16 * b + 16), v, out)
             cols.append(out)
         return cols
 
-    def gather_meta(offsets):
+    def gather_meta(offsets, only):
         out = jnp.zeros((8, 128), f32)
         for b, a in enumerate(offsets):
-            v = m1s[...] if a == 0 else m1g[0][slot_of(a, 0)]
+            if a not in only:
+                continue
+            k, i = slot_of(a, 0) if a else (0, 0)
+            v = m1s[...] if a == 0 else m1g[k, 0][i]
             out = jnp.where((lane8 >= 16 * b) & (lane8 < 16 * b + 16), pltpu.roll(v, 16 * b, 1) if b else v, out)
         return out
 
     bases1 = ((16, 48), (32, 64))
     bases2 = ((0, 64), (16, 80), (32, 96), (48, 112))
-    near_off, far_off = (-1, 0, 1), (14, 15, 16, 17, 18)
-    rot_n, sta_n = gather_cols(m1s, m1g, near_off, bases1)
-    rot_f, sta_f = gather_cols(m1s, m1g, far_off, bases1)
-    meta_n, meta_f = gather_meta(near_off), gather_meta(far_off)
-
     drift = off_s[0] - RI
     rows = row_iota((128, 128))
     lanes = lane_iota((128, 128))
@@ -245,10 +256,7 @@
         at = lanes + (drift + base) + meta[0:1, :].astype(jnp.int32)
         return jnp.where(rows == at, 1.0 - w, 0.0) + jnp.where(rows == at + 1, w, 0.0)
 
-    w_n = weights(meta_n, 16)
-    w_f = weights(meta_f, -16)
-
-    def opposite(rn, sn, rf, sf):
+    def opposite(w_n, w_f, rn, sn, rf, sf):
         flux = jnp.dot(sf, w_n, precision=HI, preferred_element_type=f32) - rn
         fluxf = jnp.dot(sn, w_f, precision=HI, preferred_element_type=f32) - rf
         back = lax.dot_general(fluxf, w_f, (((1,), (1,)), ((), ())), precision=HI, preferred_element_type=f32)
@@ -258,21 +266,23 @@
         e, w = meta[1:2, :], meta[3:4, :]
         return (1.0 - e) * (1.0 - w), (1.0 - e) * w + e * (1.0 - w), e * w
 
-    lw_n, lw_f = local_weights(meta_n), local_weights(meta_f)
-
     def spread(lw, v):
         return lw[0] * right(v) + lw[1] * v + lw[2] * left(v)
 
     def collect(lw, v):
         return left(lw[0] * v) + lw[1] * v + right(lw[2] * v)
 
-    bl0, bl1 = meta_n[4:5, :], meta_n[5:6, :]
-    eb = spread(lw_n, bl0)
-    c0 = (1.0 - 2 * DIFF) * bl0 + DIFF * (left(bl0) + right(bl0)) - ADV * (bl0 - right(bl0)) + bl1
     r32 = row_iota((32, 128))
-    for i, v in enumerate((bl0, bl1, c0, collect(lw_n, bl0), collect(lw_n, eb), eb)):
-        picked = jnp.where(lane32 == r32 + 15, jnp.broadcast_to(v, (32, 128)), 0.0)
-        bb[i] = jnp.broadcast_to(jnp.sum(picked, axis=1, keepdims=True), (32, 128))
+
+    def c0_row(bl0, bl1):
+        return (1.0 - 2 * DIFF) * bl0 + DIFF * (left(bl0) + right(bl0)) - ADV * (bl0 - right(bl0)) + bl1
+
+    def plane_coefs(meta, lw):
+        bl0, bl1 = meta[4:5, :], meta[5:6, :]
+        eb = spread(lw, bl0)
+        for i, v in enumerate((bl0, bl1, c0_row(bl0, bl1), collect(lw, bl0), collect(lw, eb), eb)):
+            picked = jnp.where(lane32 == r32 + 15, jnp.broadcast_to(v, (32, 128)), 0.0)
+            bb[i] = jnp.broadcast_to(jnp.sum(picked, axis=1, keepdims=True), (32, 128))
 
     def coef(i, q):
         return bb[i, pl.ds(q, 1), :]
@@ -292,84 +302,148 @@
     def beside(v):
         return pltpu.roll(v, 1, 0) + pltpu.roll(v, v.shape[0] - 1, 0)
 
+    def columns_at(flux, back, k):
+        ln = lane_iota(flux.shape)
+        return (jnp.where(ln == 127, pltpu.roll(flux, (127 - k) & 127, 1), 0.0),
+                jnp.where(ln == 0, pltpu.roll(back, (128 - k) & 127, 1), 0.0))
+
     def put(ref, idx, rows_, v, flux, back, k):
-        ln = lane_iota(flux.shape)
-        f = jnp.where(ln == 127, pltpu.roll(flux, 127 - k, 1), 0.0)
-        b = jnp.where(ln == 0, pltpu.roll(back, lax.rem(128 - k, 128), 1), 0.0)
+        f, b = columns_at(flux, back, k)
         ref[idx, rows_, 0:128] = v[:, 0:128]
         ref[idx, rows_, 128:256] = v[:, 128:256] + DIFF * f
         ref[idx, rows_, 256:384] = v[:, 256:384] - DIFF * b
         ref[idx, rows_, 384:512] = v[:, 384:512]
 
-    def seal(ref, n):
-        @pl.when(ax == 0)
-        def _():
-            ref[:, pl.ds(8 - n, n), :] = jnp.zeros((ref.shape[0], n, R), f32)
-
-        @pl.when(ax == NX - 1)
-        def _():
-            ref[:, pl.ds(24, n), :] = jnp.zeros((ref.shape[0], n, R), f32)
-
-    flux0, back0 = opposite(rot_n, sta_n, rot_f, sta_f)
-
-    near_arrivals(near1)
-    for c in (1, -1):
-        def act(c=c):
-            for copy in side(-c):
-                copy.wait_recv()
-        guard(c, act)
-    seal(x0, 2)
-    ally = slice(0, 32)
-
-    def step_u1(q, _):
-        v = x0[q + 1]
-        new = stencil(v, x0[q], x0[q + 2], beside(v)) + wide(coef(0, q)) * prof[...]
-        put(u1, q, ally, new, flux0, back0, q + 15)
-        return 0
-
-    lax.fori_loop(0, 18, step_u1, 0, unroll=3)
-    seal(u1, 1)
-
-    def take1(q, carry):
-        rot, sta = carry
-        a = pltpu.roll(u1[q, 8:24, 128:256], q + 16, 1)
-        b = pltpu.roll(u1[q, 8:24, 256:384], q + 15, 1)
-        return jnp.where(lane == q + 15, a, rot), jnp.where(lane == q + 15, b, sta)
-
+    def seal(ref, n, *parts):
+        def clear(row):
+            for lo, hi in parts:
+                ref[lo:hi, pl.ds(row, n), :] = jnp.zeros((hi - lo, n, R), f32)
+
+        pl.when(ax == 0)(lambda: clear(8 - n))
+        pl.when(ax == NX - 1)(lambda: clear(24))
+
+    ally, centre = slice(0, 32), slice(8, 24)
     lane = lane_iota((Z, 128))
     zero = jnp.zeros((Z, 128), f32)
-    rot1, sta1 = lax.fori_loop(0, 18, take1, (zero, zero), unroll=18)
-    flux1 = spread(lw_n, sta1) - rot1
-    back1 = collect(lw_n, flux1)
-
-    centre = slice(8, 24)
+    big = jnp.zeros((Z, R), f32)
+
+    def step_u1(q):
+        v = x0[q + 1]
+        u1[q] = stencil(v, x0[q], x0[q + 2], beside(v)) + wide(coef(0, q)) * prof[...]
+
+    def take1(q, rot, sta):
+        a = pltpu.roll(u1[q, :, 128:256], (q + 16) & 127, 1)
+        b = pltpu.roll(u1[q, :, 256:384], (q + 15) & 127, 1)
+        return jnp.where(lane32 == q + 15, a, rot), jnp.where(lane32 == q + 15, b, sta)
 
     def step_u2(j, carry):
         ls, qs, ps, a1, a2, a3, cols = carry
         v = u1[j + 1]
         new = stencil(v[8:24], u1[j, 8:24, :], u1[j + 2, 8:24, :], beside(v)[8:24]) + wide(coef(1, j + 1)) * prof[8:24, :]
-        put(fin, j, slice(0, 16), new, flux1, back1, j + 16)
-        lam = fin[j] - tg[j]
+        fin[j] = new
+        lam = new - tg[j]
         l2[j + 2, 8:24, :] = lam
         mid1, mid2 = lam[:, 128:256], lam[:, 256:384]
         for i, (t, l) in enumerate(((mid1, 126), (mid1, 127), (mid2, 0), (mid2, 1))):
             for h in range(2):
                 k = j + bases2[i][h]
-                cols = jnp.where(lane8 == k, pltpu.roll(t[8 * h : 8 * h + 8], lax.rem(k + 128 - l, 128), 1), cols)
+                cols = jnp.where(lane8 == k, pltpu.roll(t[8 * h : 8 * h + 8], (k + 128 - l) & 127, 1), cols)
         q = j + 1
         return (ls + lam * lam, qs + wide(coef(2, q)) * lam, ps + wide(coef(0, q)) * lam,
                 a1 + coef(3, q) * mid2, a2 + coef(4, q) * mid2, a3 + coef(5, q) * mid1, cols)
 
-    big = jnp.zeros((Z, R), f32)
-    ls, qs, ps, a1, a2, a3, cols = lax.fori_loop(0, J, step_u2, (big, big, big, zero, zero, zero, jnp.zeros(tile, f32)), unroll=2)
-    m2s[...] = cols
+    def local_flux(lw, rot, sta):
+        flux = spread(lw, sta) - rot
+        return flux, collect(lw, flux)
+
+    meta_o = gather_meta(near_off, (0,))
+    plane_coefs(meta_o, local_weights(meta_o))
+    seal(x0, 2, (0, 20))
+
+    def inner_u1(q, _):
+        step_u1(q)
+        return 0
+
+    lax.fori_loop(2, 16, inner_u1, 0, unroll=2)
+    seal(u1, 1, (2, 16))
+    wide0 = jnp.zeros((32, 128), f32)
+    rot1, sta1 = lax.fori_loop(2, 16, lambda q, c: take1(q, *c), (wide0, wide0), unroll=14)
+    sums = lax.fori_loop(2, 14, step_u2, (big, big, big, zero, zero, zero, jnp.zeros(tile, f32)), unroll=2)
+
+    arrivals(near1, m1g, 0, OPPOSITE)
+    rot_f, sta_f = gather_cols(m1s, m1g, far_off, far_off, bases1)
+    meta_f = gather_meta(far_off, far_off)
+    w_f, lw_f = weights(meta_f, -16), local_weights(meta_f)
+    rot_o, sta_o = gather_cols(m1s, m1g, near_off, (0,), bases1)
+
+    arrivals(near1, m1g, 0, LATE)
+    rot_e, sta_e = gather_cols(m1s, m1g, near_off, (-1, 1), bases1)
+    rot_n, sta_n = rot_o + rot_e, sta_o + sta_e
+    meta_n = meta_o + gather_meta(near_off, (-1, 1))
+    lw_n, w_n = local_weights(meta_n), weights(meta_n, 16)
+    flux0, back0 = opposite(w_n, w_f, rot_n, sta_n, rot_f, sta_f)
+    plane_coefs(meta_n, lw_n)
+    for q in (0, 1, 16, 17):
+        step_u1(q)
+    seal(u1, 1, (0, 2), (16, 18))
+    for q in (0, 1, 16, 17):
+        rot1, sta1 = take1(q, rot1, sta1)
+    for j in (0, 1, 14, 15):
+        sums = step_u2(j, sums)
+    ls, qs, ps, a1, a2, a3, cols = sums
+
+    zrow = row_iota((32, 128))
+    inside = ((zrow >= 8) | (ax != 0)) & ((zrow < 24) | (ax != NX - 1))
+    live = inside & (lane32 >= 15) & (lane32 <= 32)
+    d255 = jnp.where(live, DIFF * flux0, 0.0)
+    d256 = jnp.where(live, -DIFF * back0, 0.0)
+    flux1, back1 = local_flux(lw_n, rot1 + d255, sta1 + d256)
+
+    def pushed(d):
+        return (1.0 - 5 * DIFF - ADV) * d + DIFF * (left(d) + beside(d)) + (DIFF + ADV) * right(d)
+
+    own = (lane >= 16) & (lane < 32)
+    adds = [jnp.where(own, v[8:24], 0.0)
+            for v in (DIFF * d255, pushed(d255) + DIFF * flux1, pushed(d256) - DIFF * back1, DIFF * d256)]
+    for j in (0, 1, 14, 15, *range(2, 14)):
+        r = [pltpu.roll(v, (l - j - 16) & 127, 1) for v, l in zip(adds, (126, 127, 0, 1))]
+        add1 = jnp.where(lane == 126, r[0], jnp.where(lane == 127, r[1], 0.0))
+        add2 = jnp.where(lane == 0, r[2], jnp.where(lane == 1, r[3], 0.0))
+        l2[j + 2, 8:24, 128:256] += add1
+        l2[j + 2, 8:24, 256:384] += add2
+        fin[j, :, 128:256] += add1
+        fin[j, :, 256:384] += add2
+    more = jnp.zeros(tile, f32)
+    for i, v in enumerate(adds):
+        for h in range(2):
+            s = (bases2[i][h] - 16) & 127
+            more = more + (pltpu.roll(v[8 * h : 8 * h + 8], s, 1) if s else v[8 * h : 8 * h + 8])
+    m2s[...] = cols + more
 
     def near2(a, c):
         return near_copy(l2.at[plane_own[a], row_own[c], :], l2, a, c, 1)
 
-    for c in GROUPS:
-        send_all(near2, m2s, m2g, 1, c)
-
+    send_all(near2, m2s, m2g, 1)
+
+    bl0, bl1 = meta_n[4:5, :], meta_n[5:6, :]
+    eb = spread(lw_n, bl0)
+
+    def along(row, v):
+        return jnp.sum(row * v, axis=1, keepdims=True)
+
+    crow = c0_row(bl0, bl1)
+    for_q, for_p = [[along(r, v) for v in adds] for r in (crow, bl0)]
+
+    def fix(v, parts):
+        one, two = v[:, 128:256], v[:, 256:384]
+        one = one + jnp.where(lane == 126, parts[0], 0.0) + jnp.where(lane == 127, parts[1], 0.0)
+        two = two + jnp.where(lane == 0, parts[2], 0.0) + jnp.where(lane == 1, parts[3], 0.0)
+        return jnp.concatenate([v[:, 0:128], one, two, v[:, 384:512]], axis=1)
+
+    qs, ps = fix(qs, for_q), fix(ps, for_p)
+    a1 = a1 + along(collect(lw_n, bl0), adds[2])
+    a2 = a2 + along(collect(lw_n, eb), adds[2])
+    a3 = a3 + along(eb, adds[1])
     zr = row_iota((Z, R))
     pz = jnp.where(zr == 0, 0.0, pltpu.roll(ps, 1, 0)) + jnp.where(zr == Z - 1, 0.0, pltpu.roll(ps, Z - 1, 0))
     vv = qs + (ctr - (1.0 - 6 * DIFF - ADV) - 4 * DIFF) * ps + up * left(ps) + dn * right(ps) + DIFF * pz
@@ -386,7 +460,7 @@
     rowsum = []
     for m in range(M):
         rowsum.append(fold(bs[m] * vv) + fold(bh[0, m] * top + bh[1, m] * bot))
-    rowsum.append(fold(ls))
+    rowsum.append(fold(ls) + jnp.sum(more * (2.0 * cols + more), axis=0, keepdims=True))
     rowsum.append(jnp.zeros((7, 128), f32))
     stack = jnp.concatenate(rowsum, axis=0)
     stack = jnp.broadcast_to(jnp.sum(stack, axis=1, keepdims=True), (24, 128))
@@ -403,51 +477,65 @@
             src_ref=rrs, dst_ref=rrr.at[OTHERS.index((-x % 4, -y % 4, -z % 4, c))], send_sem=rr_ss.at[0], recv_sem=rr_rs.at[0],
             device_id=(ys[y][0] + xs[x] + zs[z], ys[y][1] + cs[c]), device_id_type=MESH).start()
 
-    arrivals(m2g, 1)
-    zrow = row_iota((32, 128))
-    inside = ((zrow >= 8) | (ax != 0)) & ((zrow < 24) | (ax != NX - 1))
+    def misfit_cols(offsets, only):
+        return [jnp.where(inside, c, 0.0) for c in gather_cols(m2s, m2g, offsets, only, bases2)]
 
     def adjoint_cols(cs, lw):
-        c254, c255, c256, c257 = [jnp.where(inside, c, 0.0) for c in cs]
-        flux = spread(lw, c256) - c255
-        back = collect(lw, flux)
+        c254, c255, c256, c257 = cs
+        flux, back = local_flux(lw, c255, c256)
 
         def one(c, out, term):
             return (1.0 - 5 * DIFF - ADV) * c + DIFF * (out + right(c) + beside(c)) + (DIFF + ADV) * left(c) + DIFF * term
 
-        return flux, back, one(c255, c254, flux), one(c256, c257, -back)
-
-    flux_n, back_n, rot_n1, sta_n1 = adjoint_cols(gather_cols(m2s, m2g, near_off, bases2), lw_n)
-    _, _, rot_f1, sta_f1 = adjoint_cols(gather_cols(m2s, m2g, far_off, bases2), lw_f)
-    fluxa, backa = opposite(rot_n1[8:24], sta_n1[8:24], rot_f1[8:24], sta_f1[8:24])
-    near_arrivals(near2)
-    seal(l2, 2)
-
-    def step_l1(q, _):
+        return flux, back, one(c255, c254, flux)[8:24], one(c256, c257, -back)[8:24]
+
+    def step_l1(q, flux, back):
         v = l2[q + 1]
         new = stencil(v, l2[q + 2], l2[q], beside(v))
-        put(l1, q, ally, new, flux_n, back_n, q + 15)
+        put(l1, q, ally, new, flux, back, q + 15)
+
+    def step_l0(j):
+        v = l1[j + 1]
+        sen[j] = stencil(v[8:24], l1[j + 2, 8:24, :], l1[j, 8:24, :], beside(v)[8:24])
+
+    arrivals(near2, m2g, 1, SAME)
+    seal(l2, 2, (0, 20))
+    cols_o = misfit_cols(near_off, (0,))
+    flux_n, back_n = local_flux(lw_n, cols_o[1], cols_o[2])
+
+    def inner_l1(q, _):
+        step_l1(q, flux_n, back_n)
         return 0
 
-    lax.fori_loop(0, 18, step_l1, 0, unroll=3)
-    seal(l1, 1)
-
-    def step_l0(j, _):
-        v = l1[j + 1]
-        new = stencil(v[8:24], l1[j + 2, 8:24, :], l1[j, 8:24, :], beside(v)[8:24])
-        put(sen, j, slice(0, 16), new, fluxa, backa, j + 16)
+    def inner_l0(j, _):
+        step_l0(j)
         return 0
 
-    lax.fori_loop(0, J, step_l0, 0, unroll=4)
+    lax.fori_loop(3, 15, inner_l1, 0, unroll=2)
+    seal(l1, 1, (3, 15))
+    lax.fori_loop(3, 13, inner_l0, 0, unroll=2)
+    arrivals(near2, m2g, 1, OPPOSITE)
+    _, _, rot_f1, sta_f1 = adjoint_cols(misfit_cols(far_off, far_off), lw_f)
+
+    arrivals(near2, m2g, 1, LATE)
+    flux_n, back_n, rot_n1, sta_n1 = adjoint_cols([o + e for o, e in zip(cols_o, misfit_cols(near_off, (-1, 1)))], lw_n)
+    fluxa, backa = opposite(w_n, w_f, rot_n1, sta_n1, rot_f1, sta_f1)
+    for q in (0, 1, 2, 15, 16, 17):
+        step_l1(q, flux_n, back_n)
+    seal(l1, 1, (0, 3), (15, 18))
+    for j in (0, 1, 2, 13, 14, 15):
+        step_l0(j)
+    for j in range(J):
+        f, b = columns_at(fluxa, backa, j + 16)
+        sen[j, :, 128:256] += DIFF * f
+        sen[j, :, 256:384] -= DIFF * b
 
     whole(rrr, rr_ss.at[0], rr_rs.at[0]).wait_recv()
     total = rrs[...] + jnp.sum(rrr[...], axis=0)
     tot[...] = jnp.broadcast_to(total, (8, 128))
 
-    near_departures(near1)
-    near_departures(near2)
-    departures(m1g, 0)
-    departures(m2g, 1)
+    departures(near1, m1g, 0)
+    departures(near2, m2g, 1)
     for c in (1, -1):
         def act(c=c):
             for copy in side(c):
@@ -483,12 +571,12 @@
             pltpu.VMEM((20, 32, R), f32), pltpu.VMEM((18, 32, R), f32),
             pltpu.VMEM((J, Z, R), f32), pltpu.VMEM((M, Z, R), f32), pltpu.VMEM((2, M, 1, R), f32),
             pltpu.VMEM((32, R), f32),
-            *[pltpu.VMEM((8, 128), f32), *[pltpu.VMEM((len(PARTNERS[c]), 8, 128), f32) for c in GROUPS]] * 2,
+            *[pltpu.VMEM((8, 128), f32), [pltpu.VMEM((len(p), 8, 128), f32) for p in PARTNERS.values()]] * 2,
             pltpu.VMEM((1, 128), f32), pltpu.VMEM((NA * NX - 1, 1, 128), f32),
             pltpu.VMEM((6, 32, 128), f32),
             pltpu.VMEM((2, J), f32), pltpu.VMEM((2, J), jnp.int32), pltpu.VMEM((2, J), f32),
             pltpu.SMEM((M,), f32), pltpu.SMEM((2,), jnp.int32),
-            dma((8,)), dma((2, 8)), dma((2, 8)), dma((2, 3)), dma((2, 3)), dma((2, 2)), dma((2, 2)), dma((1,)), dma((1,)),
+            dma((8,)), dma((2, 8)), dma((2, 8)), dma((2, 3, 3)), dma((2, 3, 3)), dma((2, 2)), dma((2, 2)), dma((1,)), dma((1,)),
             pltpu.SemaphoreType.REGULAR,
         ],
         compiler_params=pltpu.CompilerParams(collective_id=0, has_side_effects=True, vmem_limit_bytes=40 * 1024 * 1024),

time: 33.2 us -> 30.4 us (0.916)
  Pallas kernels: 32.4 us -> 29.6 us
    pallas_call x1, Pallas kernels: 30.9 us -> 28.1 us  [on_device(): pl.pallas_call(kernel, out_shape=(pltpu.VMEM((J, Z, R), f32), pltpu.VMEM(...]
where the time goes in v3:
time: 30.4 us; the launch traced here: 30.2 us
  Pallas kernels  29.6 us (97%)
  between operations  0.64 us (2%)
    pallas_call x1, Pallas kernels, on_device(): pl.pallas_call(kernel, out_shape=(pltpu.VMEM((J, Z, R), f32), pltpu.VMEM(...  28.1 us
    pallas_call x1, Pallas kernels, on_device(): pl.pallas_call(finish, out_shape=(block, block, jax.ShapeDtypeStruct((1,...  1.5 us

profile of v3, /device:TPU:1, one launch (start us, length us, event | category | flops | bytes accessed | tf_op | source)
XLA Modules:
  0.0 30.2 jit_solution(2663991629453033873)
XLA Ops:
  0.6 28.1 %shard_map.111 = (f32[16,16,512]{2,1,0:T(8,128)S(1)}, f32[16,16,512]{2,1,0:T(8,128)S(1)}, f32[8,128]{1,0:T(8,128)S(1)}) custom-call(f32[16,16,512]{2,1,0:T(8,128)} %u_h.1, f32[16,16,512]{2,1,0:T(8,128)} %t_h.1, f32[16,16,512]{2,1,0:T(8,128)} %basis_h.1, f32[16]{0:T(128)} %coef_h.1, f32[2,16]{1,0:T(2,128)} %blade_h.1, s32[2]{0:T(128)} %off_h.1, ...), custom_call_target="tpu_custom_call" | custom-call | tf_op jit(solution)/shard_map/pallas_call | solution.py:564
  28.7 1.5 %shard_map.112 = (f32[16,16,512]{2,1,0:T(8,128)}, f32[16,16,512]{2,1,0:T(8,128)}, f32[1,16]{1,0:T(1,128)}, f32[1,1]{1,0:T(1,128)}) custom-call(f32[16,16,512]{2,1,0:T(8,128)S(1)} %get-tuple-element.11.fin, f32[16,16,512]{2,1,0:T(8,128)S(1)} %get-tuple-element.12.sen, f32[8,128]{1,0:T(8,128)S(1)} %get-tuple-element.13.tot), custom_call_target="tpu_custom_call" | custom-call | tf_op jit(solution)/shard_map/pallas_call | solution.py:584

commit v4 on v3

--- a/solution.py
+++ b/solution.py
@@ -137,9 +137,9 @@
         return [n for n in NEAR if n[1] == c and (k == LATE) == (n[0] != 0)] if k != OPPOSITE else []
 
     def send_all(near_of, src, dst, n):
-        for c in GROUPS:
+        for c in (1, -1, 0):
             def act(c=c):
-                for k in range(3):
+                for k in (SAME, LATE, OPPOSITE):
                     for a, _ in near_group(k, c):
                         near_of(a, c).start()
                     for a, _ in PARTNERS.get((k, c), ()):
@@ -364,11 +364,11 @@
         step_u1(q)
         return 0
 
-    lax.fori_loop(2, 16, inner_u1, 0, unroll=2)
+    lax.fori_loop(2, 16, inner_u1, 0, unroll=7)
     seal(u1, 1, (2, 16))
     wide0 = jnp.zeros((32, 128), f32)
     rot1, sta1 = lax.fori_loop(2, 16, lambda q, c: take1(q, *c), (wide0, wide0), unroll=14)
-    sums = lax.fori_loop(2, 14, step_u2, (big, big, big, zero, zero, zero, jnp.zeros(tile, f32)), unroll=2)
+    sums = lax.fori_loop(2, 14, step_u2, (big, big, big, zero, zero, zero, jnp.zeros(tile, f32)), unroll=4)
 
     arrivals(near1, m1g, 0, OPPOSITE)
     rot_f, sta_f = gather_cols(m1s, m1g, far_off, far_off, bases1)
@@ -511,9 +511,9 @@
         step_l0(j)
         return 0
 
-    lax.fori_loop(3, 15, inner_l1, 0, unroll=2)
+    lax.fori_loop(3, 15, inner_l1, 0, unroll=4)
     seal(l1, 1, (3, 15))
-    lax.fori_loop(3, 13, inner_l0, 0, unroll=2)
+    lax.fori_loop(3, 13, inner_l0, 0, unroll=5)
     arrivals(near2, m2g, 1, OPPOSITE)
     _, _, rot_f1, sta_f1 = adjoint_cols(misfit_cols(far_off, far_off), lw_f)
 

time: 30.4 us -> 28.6 us (0.941)
  Pallas kernels: 29.6 us -> 27.9 us
    pallas_call x1, Pallas kernels: 28.1 us -> 26.4 us  [on_device(): pl.pallas_call(kernel, out_shape=(pltpu.VMEM((J, Z, R), f32), pltpu.VMEM(...]
where the time goes in v4:
time: 28.6 us; the launch traced here: 28.5 us
  Pallas kernels  27.9 us (98%)
  between operations  0.64 us (2%)
    pallas_call x1, Pallas kernels, on_device(): pl.pallas_call(kernel, out_shape=(pltpu.VMEM((J, Z, R), f32), pltpu.VMEM(...  26.4 us
    pallas_call x1, Pallas kernels, on_device(): pl.pallas_call(finish, out_shape=(block, block, jax.ShapeDtypeStruct((1,...  1.5 us

profile of v4, /device:TPU:1, one launch (start us, length us, event | category | flops | bytes accessed | tf_op | source)
XLA Modules:
  0.0 28.5 jit_solution(3687124731295930228)
XLA Ops:
  0.6 26.4 %shard_map.111 = (f32[16,16,512]{2,1,0:T(8,128)S(1)}, f32[16,16,512]{2,1,0:T(8,128)S(1)}, f32[8,128]{1,0:T(8,128)S(1)}) custom-call(f32[16,16,512]{2,1,0:T(8,128)} %u_h.1, f32[16,16,512]{2,1,0:T(8,128)} %t_h.1, f32[16,16,512]{2,1,0:T(8,128)} %basis_h.1, f32[16]{0:T(128)} %coef_h.1, f32[2,16]{1,0:T(2,128)} %blade_h.1, s32[2]{0:T(128)} %off_h.1, ...), custom_call_target="tpu_custom_call" | custom-call | tf_op jit(solution)/shard_map/pallas_call | solution.py:564
  27.0 1.5 %shard_map.112 = (f32[16,16,512]{2,1,0:T(8,128)}, f32[16,16,512]{2,1,0:T(8,128)}, f32[1,16]{1,0:T(1,128)}, f32[1,1]{1,0:T(1,128)}) custom-call(f32[16,16,512]{2,1,0:T(8,128)S(1)} %get-tuple-element.11.fin, f32[16,16,512]{2,1,0:T(8,128)S(1)} %get-tuple-element.12.sen, f32[8,128]{1,0:T(8,128)S(1)} %get-tuple-element.13.tot), custom_call_target="tpu_custom_call" | custom-call | tf_op jit(solution)/shard_map/pallas_call | solution.py:584

commit v5 on v4

--- a/solution.py
+++ b/solution.py
@@ -109,9 +109,15 @@
     m1s[4:6, 0:16] = blade_v[...]
     m1s[...] = m1s[...] + taken
 
+    for i in (4, 6):
+        loads[i].wait()
+
+    def mix(m, acc):
+        return acc + coef_s[m] * bs[m]
+
+    prof[8:24, :] = lax.fori_loop(0, M, mix, jnp.zeros((Z, R), f32), unroll=4)
+
     pl.semaphore_wait(barrier, len(GREETED))
-    plane_src = {-1: pl.ds(0, 2), 0: pl.ds(0, 16), 1: pl.ds(14, 2)}
-    row_src = {-1: pl.ds(0, 2), 0: pl.ds(0, 16), 1: pl.ds(14, 2)}
     plane_dst = {-1: pl.ds(18, 2), 0: pl.ds(2, 16), 1: pl.ds(0, 2)}
     row_dst = {-1: pl.ds(24, 2), 0: pl.ds(8, 16), 1: pl.ds(6, 2)}
     plane_own = {-1: pl.ds(2, 2), 0: pl.ds(2, 16), 1: pl.ds(16, 2)}
@@ -150,20 +156,7 @@
     m2g = dict(zip(PARTNERS, m2r))
 
     def near1(a, c):
-        return near_copy(u_h.at[plane_src[a], row_src[c], :], x0, a, c, 0)
-
-    send_all(near1, m1s, m1g, 0)
-
-    for a, c in GREETED:
-        pl.semaphore_signal(ready, inc=1, device_id=partner(a, c), device_id_type=MESH)
-
-    for c in loads[4:]:
-        c.wait()
-
-    def mix(m, acc):
-        return acc + coef_s[m] * bs[m]
-
-    prof[8:24, :] = lax.fori_loop(0, M, mix, jnp.zeros((Z, R), f32), unroll=4)
+        return near_copy(x0.at[plane_own[a], row_own[c], :], x0, a, c, 0)
 
     def side(c):
         i, src, dst = (0, 23, 7) if c > 0 else (1, 8, 24)
@@ -173,16 +166,24 @@
                 send_sem=side_ss.at[0, i], recv_sem=side_rs.at[0, i],
                 device_id=partner(0, c), device_id_type=MESH),
             pltpu.make_async_remote_copy(
-                src_ref=basis_h.at[:, pl.ds(src - 8, 1), :], dst_ref=bh.at[i],
+                src_ref=bs.at[:, pl.ds(src - 8, 1), :], dst_ref=bh.at[i],
                 send_sem=side_ss.at[1, i], recv_sem=side_rs.at[1, i],
                 device_id=partner(0, c), device_id_type=MESH),
         )
 
     for c in (1, -1):
-        def act(c=c):
-            for copy in side(c):
-                copy.start()
-        guard(c, act)
+        guard(c, lambda c=c: side(c)[0].start() and None)
+
+    send_all(near1, m1s, m1g, 0)
+    for c in (1, -1):
+        guard(c, lambda c=c: side(c)[1].start() and None)
+
+
+    for a, c in GREETED:
+        pl.semaphore_signal(ready, inc=1, device_id=partner(a, c), device_id_type=MESH)
+
+    for i in (5, 7):
+        loads[i].wait()
 
     def whole(ref, ss, rs):
         return pltpu.make_async_remote_copy(
@@ -209,10 +210,7 @@
 
     arrivals(near1, m1g, 0, SAME)
     for c in (1, -1):
-        def act(c=c):
-            for copy in side(-c):
-                copy.wait_recv()
-        guard(c, act)
+        guard(c, lambda c=c: side(-c)[0].wait_recv() and None)
     lane32 = lane_iota((32, 128))
 
     near_off, far_off = (-1, 0, 1), (14, 15, 16, 17, 18)
@@ -424,6 +422,9 @@
         return near_copy(l2.at[plane_own[a], row_own[c], :], l2, a, c, 1)
 
     send_all(near2, m2s, m2g, 1)
+
+    for c in (1, -1):
+        guard(c, lambda c=c: side(-c)[1].wait_recv() and None)
 
     bl0, bl1 = meta_n[4:5, :], meta_n[5:6, :]
     eb = spread(lw_n, bl0)

time: 28.6 us -> 28 us (0.979)
  Pallas kernels: 27.9 us -> 27.3 us
    pallas_call x1, Pallas kernels: 26.4 us -> 25.8 us  [on_device(): pl.pallas_call(kernel, out_shape=(pltpu.VMEM((J, Z, R), f32), pltpu.VMEM(...]
where the time goes in v5:
time: 28 us; the launch traced here: 27.9 us
  Pallas kernels  27.3 us (98%)
  between operations  0.64 us (2%)
    pallas_call x1, Pallas kernels, on_device(): pl.pallas_call(kernel, out_shape=(pltpu.VMEM((J, Z, R), f32), pltpu.VMEM(...  25.8 us
    pallas_call x1, Pallas kernels, on_device(): pl.pallas_call(finish, out_shape=(block, block, jax.ShapeDtypeStruct((1,...  1.5 us

profile of v5, /device:TPU:1, one launch (start us, length us, event | category | flops | bytes accessed | tf_op | source)
XLA Modules:
  0.0 27.9 jit_solution(2524457682252990565)
XLA Ops:
  0.6 25.8 %shard_map.111 = (f32[16,16,512]{2,1,0:T(8,128)S(1)}, f32[16,16,512]{2,1,0:T(8,128)S(1)}, f32[8,128]{1,0:T(8,128)S(1)}) custom-call(f32[16,16,512]{2,1,0:T(8,128)} %u_h.1, f32[16,16,512]{2,1,0:T(8,128)} %t_h.1, f32[16,16,512]{2,1,0:T(8,128)} %basis_h.1, f32[16]{0:T(128)} %coef_h.1, f32[2,16]{1,0:T(2,128)} %blade_h.1, s32[2]{0:T(128)} %off_h.1, ...), custom_call_target="tpu_custom_call" | custom-call | tf_op jit(solution)/shard_map/pallas_call | solution.py:565
  26.4 1.5 %shard_map.112 = (f32[16,16,512]{2,1,0:T(8,128)}, f32[16,16,512]{2,1,0:T(8,128)}, f32[1,16]{1,0:T(1,128)}, f32[1,1]{1,0:T(1,128)}) custom-call(f32[16,16,512]{2,1,0:T(8,128)S(1)} %get-tuple-element.11.fin, f32[16,16,512]{2,1,0:T(8,128)S(1)} %get-tuple-element.12.sen, f32[8,128]{1,0:T(8,128)S(1)} %get-tuple-element.13.tot), custom_call_target="tpu_custom_call" | custom-call | tf_op jit(solution)/shard_map/pallas_call | solution.py:585

commit v6 on v5

--- a/solution.py
+++ b/solution.py
@@ -25,7 +25,10 @@
     (k, g): [(a, c) for a, c in NEAR + FAR if c == g and k == (OPPOSITE if a > 1 else LATE if a else SAME)]
     for k in range(3) for g in GROUPS if (k, g) != (SAME, 0)
 }
-GREETED = NEAR + FAR + [(6, 0), (6, 2), (-6, 0), (-6, 2)]
+ALWAYS = [(-1, 0), (1, 0), (0, -1), (0, 1)] + [(a, 0) for a in range(14, 19)] + [(16, -1), (16, 1)]
+ALWAYS += [(a, c) for a in (-8, -4, 4, 8) for c in (0, 2)]
+INSIDE = [-1, 1, 14, 15, 17, 18]
+AROUND = [-4, 4]
 OTHERS = sorted(
     [(x, y, z, c) for x in range(4) for y in range(4) for z in range(4) for c in range(2) if x + y + z + c],
     key=lambda o: -(sum(v > 0 for v in o[:3]) * 8 + sum(v == 2 for v in o[:3])),
@@ -84,8 +87,27 @@
     loads[0].start()
     barrier = pltpu.get_barrier_semaphore()
 
-    for a, c in GREETED:
-        pl.semaphore_signal(barrier, inc=1, device_id=partner(a, c), device_id_type=MESH)
+    def greet(sem):
+        def signal(a, c):
+            pl.semaphore_signal(sem, inc=1, device_id=partner(a, c), device_id_type=MESH)
+
+        for a, c in ALWAYS:
+            signal(a, c)
+        for c in (1, -1):
+            at_end = ax == (NX - 1 if c > 0 else 0)
+
+            @pl.when(at_end)
+            def _(c=c):
+                for a in AROUND:
+                    signal(a, c)
+
+            @pl.when(jnp.logical_not(at_end))
+            def _(c=c):
+                for a in INSIDE:
+                    signal(a, c)
+
+    greeted = len(ALWAYS) + 2 * len(INSIDE) - jnp.where((ax == 0) | (ax == NX - 1), len(INSIDE) - len(AROUND), 0)
+    greet(barrier)
     for c in loads[1:]:
         c.start()
 
@@ -117,7 +139,7 @@
 
     prof[8:24, :] = lax.fori_loop(0, M, mix, jnp.zeros((Z, R), f32), unroll=4)
 
-    pl.semaphore_wait(barrier, len(GREETED))
+    pl.semaphore_wait(barrier, greeted)
     plane_dst = {-1: pl.ds(18, 2), 0: pl.ds(2, 16), 1: pl.ds(0, 2)}
     row_dst = {-1: pl.ds(24, 2), 0: pl.ds(8, 16), 1: pl.ds(6, 2)}
     plane_own = {-1: pl.ds(2, 2), 0: pl.ds(2, 16), 1: pl.ds(16, 2)}
@@ -179,8 +201,7 @@
         guard(c, lambda c=c: side(c)[1].start() and None)
 
 
-    for a, c in GREETED:
-        pl.semaphore_signal(ready, inc=1, device_id=partner(a, c), device_id_type=MESH)
+    greet(ready)
 
     for i in (5, 7):
         loads[i].wait()
@@ -467,7 +488,7 @@
     stack = jnp.broadcast_to(jnp.sum(stack, axis=1, keepdims=True), (24, 128))
     rrs[...] = jnp.sum(jnp.where(row_iota((24, 128)) == lane_iota((24, 128)), stack, 0.0), axis=0, keepdims=True)
 
-    pl.semaphore_wait(ready, len(GREETED))
+    pl.semaphore_wait(ready, greeted)
     px, pz_, py, pc = (az >> 2) & 3, az & 3, (ax >> 1) * 2 + (az >> 4), ax & 1
     xs = [((px + d) & 3) << 2 for d in range(4)]
     zs = [(pz_ + d) & 3 for d in range(4)]

time: 28 us -> 27.6 us (0.986)
  Pallas kernels: 27.3 us -> 26.8 us
    pallas_call x1, Pallas kernels: 25.8 us -> 25.3 us  [on_device(): pl.pallas_call(kernel, out_shape=(pltpu.VMEM((J, Z, R), f32), pltpu.VMEM(...]
where the time goes in v6:
time: 27.6 us; the launch traced here: 27.5 us
  Pallas kernels  26.8 us (97%)
  between operations  0.64 us (2%)
    pallas_call x1, Pallas kernels, on_device(): pl.pallas_call(kernel, out_shape=(pltpu.VMEM((J, Z, R), f32), pltpu.VMEM(...  25.3 us
    pallas_call x1, Pallas kernels, on_device(): pl.pallas_call(finish, out_shape=(block, block, jax.ShapeDtypeStruct((1,...  1.5 us

profile of v6, /device:TPU:1, one launch (start us, length us, event | category | flops | bytes accessed | tf_op | source)
XLA Modules:
  0.0 27.5 jit_solution(1032683441780729066)
XLA Ops:
  0.6 25.3 %shard_map.111 = (f32[16,16,512]{2,1,0:T(8,128)S(1)}, f32[16,16,512]{2,1,0:T(8,128)S(1)}, f32[8,128]{1,0:T(8,128)S(1)}) custom-call(f32[16,16,512]{2,1,0:T(8,128)} %u_h.1, f32[16,16,512]{2,1,0:T(8,128)} %t_h.1, f32[16,16,512]{2,1,0:T(8,128)} %basis_h.1, f32[16]{0:T(128)} %coef_h.1, f32[2,16]{1,0:T(2,128)} %blade_h.1, s32[2]{0:T(128)} %off_h.1, ...), custom_call_target="tpu_custom_call" | custom-call | tf_op jit(solution)/shard_map/pallas_call | solution.py:586
  26.0 1.5 %shard_map.112 = (f32[16,16,512]{2,1,0:T(8,128)}, f32[16,16,512]{2,1,0:T(8,128)}, f32[1,16]{1,0:T(1,128)}, f32[1,1]{1,0:T(1,128)}) custom-call(f32[16,16,512]{2,1,0:T(8,128)S(1)} %get-tuple-element.11.fin, f32[16,16,512]{2,1,0:T(8,128)S(1)} %get-tuple-element.12.sen, f32[8,128]{1,0:T(8,128)S(1)} %get-tuple-element.13.tot), custom_call_target="tpu_custom_call" | custom-call | tf_op jit(solution)/shard_map/pallas_call | solution.py:606

commit v7 on v6

--- a/solution.py
+++ b/solution.py
@@ -29,10 +29,13 @@
 ALWAYS += [(a, c) for a in (-8, -4, 4, 8) for c in (0, 2)]
 INSIDE = [-1, 1, 14, 15, 17, 18]
 AROUND = [-4, 4]
-OTHERS = sorted(
-    [(x, y, z, c) for x in range(4) for y in range(4) for z in range(4) for c in range(2) if x + y + z + c],
-    key=lambda o: -(sum(v > 0 for v in o[:3]) * 8 + sum(v == 2 for v in o[:3])),
-)
+def hops(t):
+    az, ax = t // NX, t % NX
+    at = ((az >> 2) & 3, az & 3, (ax >> 1) * 2 + (az >> 4))
+    return sum(v > 0 for v in at) * 4 + sum(min(v, 4 - v) for v in at), t
+
+
+TARGETS = sorted(range(NA * NX), key=hops)
 
 
 def slot_of(a, c):
@@ -383,11 +386,11 @@
         step_u1(q)
         return 0
 
-    lax.fori_loop(2, 16, inner_u1, 0, unroll=7)
+    lax.fori_loop(2, 16, inner_u1, 0, unroll=14)
     seal(u1, 1, (2, 16))
     wide0 = jnp.zeros((32, 128), f32)
     rot1, sta1 = lax.fori_loop(2, 16, lambda q, c: take1(q, *c), (wide0, wide0), unroll=14)
-    sums = lax.fori_loop(2, 14, step_u2, (big, big, big, zero, zero, zero, jnp.zeros(tile, f32)), unroll=4)
+    sums = lax.fori_loop(2, 14, step_u2, (big, big, big, zero, zero, zero, jnp.zeros(tile, f32)), unroll=6)
 
     arrivals(near1, m1g, 0, OPPOSITE)
     rot_f, sta_f = gather_cols(m1s, m1g, far_off, far_off, bases1)
@@ -489,15 +492,14 @@
     rrs[...] = jnp.sum(jnp.where(row_iota((24, 128)) == lane_iota((24, 128)), stack, 0.0), axis=0, keepdims=True)
 
     pl.semaphore_wait(ready, greeted)
-    px, pz_, py, pc = (az >> 2) & 3, az & 3, (ax >> 1) * 2 + (az >> 4), ax & 1
-    xs = [((px + d) & 3) << 2 for d in range(4)]
-    zs = [(pz_ + d) & 3 for d in range(4)]
-    ys = [(((py + d) & 1) << 4, (((py + d) >> 1) & 1) << 1) for d in range(4)]
-    cs = [pc, 1 - pc]
-    for x, y, z, c in OTHERS:
-        pltpu.make_async_remote_copy(
-            src_ref=rrs, dst_ref=rrr.at[OTHERS.index((-x % 4, -y % 4, -z % 4, c))], send_sem=rr_ss.at[0], recv_sem=rr_rs.at[0],
-            device_id=(ys[y][0] + xs[x] + zs[z], ys[y][1] + cs[c]), device_id_type=MESH).start()
+    me = az * NX + ax
+    rrr[me] = rrs[...]
+    for t in TARGETS:
+        @pl.when(me != t)
+        def _(t=t):
+            pltpu.make_async_remote_copy(
+                src_ref=rrs, dst_ref=rrr.at[me], send_sem=rr_ss.at[0], recv_sem=rr_rs.at[0],
+                device_id=(t // NX, t % NX), device_id_type=MESH).start()
 
     def misfit_cols(offsets, only):
         return [jnp.where(inside, c, 0.0) for c in gather_cols(m2s, m2g, offsets, only, bases2)]
@@ -552,8 +554,9 @@
         sen[j, :, 128:256] += DIFF * f
         sen[j, :, 256:384] -= DIFF * b
 
-    whole(rrr, rr_ss.at[0], rr_rs.at[0]).wait_recv()
-    total = rrs[...] + jnp.sum(rrr[...], axis=0)
+    others = rrr.at[pl.ds(0, NA * NX - 1)]
+    whole(others, rr_ss.at[0], rr_rs.at[0]).wait_recv()
+    total = jnp.sum(rrr[...], axis=0)
     tot[...] = jnp.broadcast_to(total, (8, 128))
 
     departures(near1, m1g, 0)
@@ -563,7 +566,7 @@
             for copy in side(c):
                 copy.wait_send()
         guard(c, act)
-    whole(rrr, rr_ss.at[0], rr_rs.at[0]).wait_send()
+    whole(others, rr_ss.at[0], rr_rs.at[0]).wait_send()
 
 
 def finish(fin, sen, tot, fin_o, sen_o, grad_o, loss_o, sems):
@@ -594,7 +597,7 @@
             pltpu.VMEM((J, Z, R), f32), pltpu.VMEM((M, Z, R), f32), pltpu.VMEM((2, M, 1, R), f32),
             pltpu.VMEM((32, R), f32),
             *[pltpu.VMEM((8, 128), f32), [pltpu.VMEM((len(p), 8, 128), f32) for p in PARTNERS.values()]] * 2,
-            pltpu.VMEM((1, 128), f32), pltpu.VMEM((NA * NX - 1, 1, 128), f32),
+            pltpu.VMEM((1, 128), f32), pltpu.VMEM((NA * NX, 1, 128), f32),
             pltpu.VMEM((6, 32, 128), f32),
             pltpu.VMEM((2, J), f32), pltpu.VMEM((2, J), jnp.int32), pltpu.VMEM((2, J), f32),
             pltpu.SMEM((M,), f32), pltpu.SMEM((2,), jnp.int32),

time: 27.6 us -> 27.6 us (level)
  no operation moved by 1% of the time
where the time goes in v7:
time: 27.6 us; the launch traced here: 27.5 us
  Pallas kernels  26.8 us (97%)
  between operations  0.64 us (2%)
    pallas_call x1, Pallas kernels, on_device(): pl.pallas_call(kernel, out_shape=(pltpu.VMEM((J, Z, R), f32), pltpu.VMEM(...  25.3 us
    pallas_call x1, Pallas kernels, on_device(): pl.pallas_call(finish, out_shape=(block, block, jax.ShapeDtypeStruct((1,...  1.5 us

profile of v7, /device:TPU:1, one launch (start us, length us, event | category | flops | bytes accessed | tf_op | source)
XLA Modules:
  0.0 27.5 jit_solution(2708806988755269202)
XLA Ops:
  0.6 25.3 %shard_map.111 = (f32[16,16,512]{2,1,0:T(8,128)S(1)}, f32[16,16,512]{2,1,0:T(8,128)S(1)}, f32[8,128]{1,0:T(8,128)S(1)}) custom-call(f32[16,16,512]{2,1,0:T(8,128)} %u_h.1, f32[16,16,512]{2,1,0:T(8,128)} %t_h.1, f32[16,16,512]{2,1,0:T(8,128)} %basis_h.1, f32[16]{0:T(128)} %coef_h.1, f32[2,16]{1,0:T(2,128)} %blade_h.1, s32[2]{0:T(128)} %off_h.1, ...), custom_call_target="tpu_custom_call" | custom-call | tf_op jit(solution)/shard_map/pallas_call | solution.py:589
  26.0 1.5 %shard_map.112 = (f32[16,16,512]{2,1,0:T(8,128)}, f32[16,16,512]{2,1,0:T(8,128)}, f32[1,16]{1,0:T(1,128)}, f32[1,1]{1,0:T(1,128)}) custom-call(f32[16,16,512]{2,1,0:T(8,128)S(1)} %get-tuple-element.11.fin, f32[16,16,512]{2,1,0:T(8,128)S(1)} %get-tuple-element.12.sen, f32[8,128]{1,0:T(8,128)S(1)} %get-tuple-element.13.tot), custom_call_target="tpu_custom_call" | custom-call | tf_op jit(solution)/shard_map/pallas_call | solution.py:609
